TPU v7x, 32 devices: a whole 2x2x4 slice. The times are simulated.
32 devices in a mesh: gx: 16 (over z, y, x), gy: 2 (over core).
Axes of the slice: x: 2, y: 2, z: 4, core: 2. Of those that a mesh axis runs over, the one named last changes fastest.
Arguments:
- rhs: float32 [16, 2, 128, 128], P('gx', 'gy'), may hold values from -57 to 57
- face_rows: int32 [16, 2, 4, 128], P('gx', 'gy'), may hold values from 0 to 127
- margin_weight: float32 [16, 2, 4, 128], P('gx', 'gy'), may hold values from 0.2 to 1
- local_blocks: bfloat16 [16, 2, 1, 128, 128], P('gx', 'gy'), may hold values from -0.4 to 4.4
- subdomain_inverse: bfloat16 [16, 2, 128, 640], P('gx', 'gy'), may hold values from -0.4 to 1.8
- coarse_basis: bfloat16 [16, 2, 128, 32], P('gx', 'gy'), may hold values from -0.5 to 0.5
- coarse_inverse: bfloat16 [16, 2, 32, 1024], P('gx', 'gy'), may hold values from -0.390625 to 0.390625
- coarse_map: int32 [32], replicated, may hold values from 0 to 31, each once
Outputs:
- solution: float32 [16, 2, 128, 128], P('gx', 'gy')
- relative_residual: float32 [128], replicated
Inputs may be any that keep to these rules, and one draw needn't show every extreme that they name: `face_rows`: rows of the subdomain, repeats possible. `coarse_map`: every position once.
All inputs are finite; a program needn't handle non-finite values.
Results may differ from a plain program's by a relative error of at most 0.004.
Values may be sent and summed in bfloat16 or wider, within the bound.
A program may use at most 64 MiB of HBM per device.

v0:
```python
import jax
import jax.numpy as jnp
from jax import lax
from jax.sharding import PartitionSpec as P

EPSILON = 1e-06


def padded(shard, sides, width):
    for axis, dim in sides:
        count, length = (lax.axis_size(axis), shard.shape[dim])
        up = [(i, (i + 1) % count) for i in range(count - 1)]
        down = [(j, i) for i, j in up]
        last = lax.slice_in_dim(shard, length - width, length, axis=dim)
        initial = lax.slice_in_dim(shard, 0, width, axis=dim)
        before = lax.ppermute(last, axis, up)
        after = lax.ppermute(initial, axis, down)
        shard = jnp.concatenate([before, shard, after], axis=dim)
    return shard


def least_squares(scale_norm, first_dot, first_norm, cross_dot, second_dot, second_norm):
    radius_one = jnp.sqrt(first_dot * first_dot + first_norm * first_norm)
    cosine_one = first_dot / radius_one
    sine_one = first_norm / radius_one
    upper_entry = cosine_one * cross_dot + sine_one * second_dot
    lower_entry = cosine_one * second_dot - sine_one * cross_dot
    radius_two = jnp.sqrt(lower_entry * lower_entry + second_norm * second_norm)
    cosine_two = lower_entry / radius_two
    sine_two = second_norm / radius_two
    weight_two = -cosine_two * sine_one * scale_norm / radius_two
    weight_one = (cosine_one * scale_norm - upper_entry * weight_two) / radius_one
    return (weight_one, weight_two, sine_one * sine_two)


def on_device(
    rhs,
    face_rows,
    margin_weight,
    local_blocks,
    subdomain_inverse,
    coarse_basis,
    coarse_inverse,
    coarse_map,
):
    right_side = rhs[0, 0]
    margin_rows = face_rows[0, 0]
    margin_weights = margin_weight[0, 0]
    local_block = local_blocks[0, 0]
    inverse_rows = subdomain_inverse[0, 0]
    basis = coarse_basis[0, 0]
    coarse_rows = coarse_inverse[0, 0]
    owned_rows = right_side.shape[0]
    system_count = right_side.shape[1]
    basis_count = basis.shape[1]
    block_rows = local_block.shape[1]
    positions = (
        coarse_map[:, None] * basis_count + jnp.arange(basis_count, dtype=jnp.int32)[None, :]
    ).reshape(-1)
    permuted = jnp.take(coarse_rows, positions, axis=1)

    def neighbour_margin(rounded):
        face_packs = rounded[margin_rows]
        along_first = padded(face_packs[0:2], (("gx", 0),), 1)
        along_second = padded(face_packs[2:4], (("gy", 0),), 1)
        return jnp.stack([along_first[0], along_first[3], along_second[0], along_second[3]], axis=0)

    def add_piece(shard_rows):
        return jnp.dot(permuted, shard_rows, preferred_element_type=jnp.float32)

    def precondition(vector):
        rounded = vector.astype(jnp.bfloat16)
        extended = jnp.concatenate(
            [rounded, neighbour_margin(rounded).reshape(-1, system_count)], axis=0
        )
        local_part = jnp.dot(inverse_rows, extended, preferred_element_type=jnp.float32)
        residual = lax.dot_general(
            basis, rounded, (((0,), (0,)), ((), ())), preferred_element_type=jnp.float32
        ).astype(jnp.bfloat16)
        solved = add_piece(lax.all_gather(residual, ("gx", "gy"), axis=0, tiled=True))
        return local_part + jnp.dot(
            basis, solved.astype(jnp.bfloat16), preferred_element_type=jnp.float32
        )

    def apply_operator(vector):
        rounded = vector.astype(jnp.bfloat16)
        own_part = jnp.einsum(
            "brc,bcn->brn",
            local_block,
            rounded.reshape(-1, block_rows, system_count),
            preferred_element_type=jnp.float32,
        ).reshape(owned_rows, system_count)
        weighted = margin_weights[:, :, None] * neighbour_margin(rounded).astype(jnp.float32)
        coupling = (
            jnp.zeros((owned_rows, system_count), jnp.float32)
            .at[margin_rows.reshape(-1)]
            .add(weighted.reshape(-1, system_count))
        )
        return own_part - coupling

    def column_norm(vector):
        squares = lax.psum(jnp.sum(vector * vector, axis=0), ("gx", "gy"))
        return jnp.sqrt(squares + EPSILON)

    def project_single(vector, direction):
        return lax.psum(jnp.sum(vector * direction, axis=0), ("gx", "gy"))

    scale_norm = column_norm(right_side)
    krylov_one = right_side / scale_norm
    precond_one = precondition(krylov_one)
    applied = apply_operator(precond_one)
    first_dot = project_single(applied, krylov_one)
    remainder = applied - first_dot * krylov_one
    first_norm = column_norm(remainder)
    krylov_two = remainder / first_norm
    precond_two = precondition(krylov_two)
    applied = apply_operator(precond_two)
    cross_dot = project_single(applied, krylov_one)
    remainder = applied - cross_dot * krylov_one
    second_dot = project_single(remainder, krylov_two)
    remainder = remainder - second_dot * krylov_two
    second_norm = column_norm(remainder)
    weight_one, weight_two, relative = least_squares(
        scale_norm, first_dot, first_norm, cross_dot, second_dot, second_norm
    )
    solution = weight_one * precond_one + weight_two * precond_two
    return (solution[None, None], relative)


def solution(mesh):
    return jax.shard_map(
        on_device,
        mesh=mesh,
        in_specs=(
            P("gx", "gy", None, None),
            P("gx", "gy", None, None),
            P("gx", "gy", None, None),
            P("gx", "gy", None, None, None),
            P("gx", "gy", None, None),
            P("gx", "gy", None, None),
            P("gx", "gy", None, None),
            P(),
        ),
        out_specs=(P("gx", "gy", None, None), P()),
        check_vma=False,
    )
```

profile of v0, /device:TPU:0, one launch (start us, length us, event | category | flops | bytes accessed | tf_op | source)
XLA Modules:
  0.0 376.9 jit_solution(13059795987256753059)
XLA Ops:
  1.6 42.0 %psum.42 = f32[128]{0:T(128)S(1)} all-reduce(f32[128]{0:T(128)S(1)} %fusion.18), channel_id=1, replica_groups=mesh['gx'=16,'gy'=2] {'gx','gy'}, use_global_device_ids=true, to_apply=%region_1.2 | all-reduce | flops 128 | bytes 1024 | tf_op jit(solution)/shard_map/psum | solution.py:102
  43.7 1.3 gather_fusion
  45.0 4.2 %collective-permute-start = (bf16[1,128,128]{2,1,0:T(8,128)(2,1)S(1)}, bf16[1,128,128]{2,1,0:T(8,128)(2,1)S(1)}, u32[]{:S(2)}, u32[]{:S(2)}) collective-permute-start(bf16[1,128,128]{2,1,0:T(8,128)(2,1)S(1)} %get-tuple-element.23), channel_id=1, source_target_pairs={{0,2},{2,4},{4,6},{6,8},{8,10},{10,12},{12,14},{14,16},{16,18},{18... | collective-permute-start | bytes 98312 | tf_op jit(solution)/shard_map/ppermute | solution.py:16
  49.2 1.3 collective-permute-start.2
  50.5 1.3 collective-permute-start.1
  51.8 1.3 collective-permute-start.3
  54.2 41.3 %all_gather.6 = bf16[1024,128]{1,0:T(8,128)(2,1)S(1)} all-gather(bf16[32,128]{1,0:T(8,128)(2,1)S(1)} %fusion.2), channel_id=1, replica_groups=mesh['gx'=16,'gy'=2] {'gx','gy'}, dimensions={0}, use_global_device_ids=true | all-gather | bytes 270336 | tf_op jit(solution)/shard_map/all_gather | solution.py:80
  95.6 3.2 gather_fusion.1
  99.9 1.3 gather_fusion.2
  101.2 1.3 collective-permute-start.4
  102.5 2.2 collective-permute-start.6
  104.8 1.3 collective-permute-start.5
  106.1 1.3 collective-permute-start.7
  107.4 3.2 collective-permute-done.5
  111.3 2.4 scatter_custom_fusion
  113.9 36.9 %psum.43 = f32[128]{0:T(128)S(1)} all-reduce(f32[128]{0:T(128)S(1)} %get-tuple-element.27), channel_id=1, replica_groups=mesh['gx'=16,'gy'=2] {'gx','gy'}, use_global_device_ids=true, to_apply=%region_4.5 | all-reduce | flops 128 | bytes 1024 | tf_op jit(solution)/shard_map/psum | solution.py:106
  150.8 42.1 %psum.44 = f32[128]{0:T(128)S(1)} all-reduce(f32[128]{0:T(128)S(1)} %multiply_reduce_fusion.3), channel_id=1, replica_groups=mesh['gx'=16,'gy'=2] {'gx','gy'}, use_global_device_ids=true, to_apply=%region_6.7 | all-reduce | flops 128 | bytes 1024 | tf_op jit(solution)/shard_map/psum | solution.py:102
  193.1 1.3 gather_fusion.3
  194.5 4.2 %collective-permute-start.8 = (bf16[1,128,128]{2,1,0:T(8,128)(2,1)S(1)}, bf16[1,128,128]{2,1,0:T(8,128)(2,1)S(1)}, u32[]{:S(2)}, u32[]{:S(2)}) collective-permute-start(bf16[1,128,128]{2,1,0:T(8,128)(2,1)S(1)} %get-tuple-element.15), channel_id=1, source_target_pairs={{0,2},{2,4},{4,6},{6,8},{8,10},{10,12},{12,14},{14,16},{16,18},{18... | collective-permute-start | bytes 98312 | tf_op jit(solution)/shard_map/ppermute | solution.py:16
  198.6 1.3 collective-permute-start.10
  199.9 1.3 collective-permute-start.9
  201.2 1.3 collective-permute-start.11
  202.5 40.9 %all_gather.7 = bf16[1024,128]{1,0:T(8,128)(2,1)S(1)} all-gather(bf16[32,128]{1,0:T(8,128)(2,1)S(1)} %fusion.3), channel_id=1, replica_groups=mesh['gx'=16,'gy'=2] {'gx','gy'}, dimensions={0}, use_global_device_ids=true | all-gather | bytes 270336 | tf_op jit(solution)/shard_map/all_gather | solution.py:80
  244.4 1.3 gather_fusion.4
  247.1 2.2 collective-permute-start.14
  249.3 1.3 collective-permute-start.13
  250.6 1.3 collective-permute-start.15
  251.9 3.2 collective-permute-done.13
  255.2 2.4 scatter_custom_fusion.1
  257.7 36.9 %psum.45 = f32[128]{0:T(128)S(1)} all-reduce(f32[128]{0:T(128)S(1)} %get-tuple-element.29), channel_id=1, replica_groups=mesh['gx'=16,'gy'=2] {'gx','gy'}, use_global_device_ids=true, to_apply=%region_9.10 | all-reduce | flops 128 | bytes 1024 | tf_op jit(solution)/shard_map/psum | solution.py:106
  294.7 42.1 %psum.46 = f32[128]{0:T(128)S(1)} all-reduce(f32[128]{0:T(128)S(1)} %multiply_reduce_fusion.1), channel_id=1, replica_groups=mesh['gx'=16,'gy'=2] {'gx','gy'}, use_global_device_ids=true, to_apply=%region_11.12 | all-reduce | flops 128 | bytes 1024 | tf_op jit(solution)/shard_map/psum | solution.py:106
  336.8 38.7 %psum.47 = f32[128]{0:T(128)S(1)} all-reduce(f32[128]{0:T(128)S(1)} %multiply_reduce_fusion), channel_id=1, replica_groups=mesh['gx'=16,'gy'=2] {'gx','gy'}, use_global_device_ids=true, to_apply=%region_13.14 | all-reduce | flops 128 | bytes 1024 | tf_op jit(solution)/shard_map/psum | solution.py:102
  (74 shorter events, 8.2 us)
Async XLA Ops:
  0.6 98.3 %copy-start = (bf16[1,1,128,640]{3,2,1,0:T(8,128)(2,1)S(1)}, bf16[1,1,128,640]{3,2,1,0:T(8,128)(2,1)}, u32[]{:S(2)}) copy-start(bf16[1,1,128,640]{3,2,1,0:T(8,128)(2,1)} %param.12) | copy-start | bytes 491524
  0.6 43.0 %copy-start.1 = (f32[1,1,128,128]{3,2,1,0:T(8,128)S(1)}, f32[1,1,128,128]{3,2,1,0:T(8,128)}, u32[]{:S(2)}) copy-start(f32[1,1,128,128]{3,2,1,0:T(8,128)} %param.8) | copy-start | bytes 196612
  1.6 42.0 %copy-start.6 = (s32[1,1,4,128]{3,2,1,0:T(4,128)S(1)}, s32[1,1,4,128]{3,2,1,0:T(4,128)}, u32[]{:S(2)}) copy-start(s32[1,1,4,128]{3,2,1,0:T(4,128)} %param.9) | copy-start | bytes 6148
  45.0 53.8 %collective-permute-start = (bf16[1,128,128]{2,1,0:T(8,128)(2,1)S(1)}, bf16[1,128,128]{2,1,0:T(8,128)(2,1)S(1)}, u32[]{:S(2)}, u32[]{:S(2)}) collective-permute-start(bf16[1,128,128]{2,1,0:T(8,128)(2,1)S(1)} %get-tuple-element.23), channel_id=1, source_target_pairs={{0,2},{2,4},{4,6},{6,8},{8,10},{10,12},{12,14},{14,16},{16,18},{18... | collective-permute-start | bytes 98312 | tf_op jit(solution)/shard_map/ppermute | solution.py:16
  49.2 49.6 %collective-permute-start.2 = (bf16[1,128,128]{2,1,0:T(8,128)(2,1)S(1)}, bf16[1,128,128]{2,1,0:T(8,128)(2,1)S(1)}, u32[]{:S(2)}, u32[]{:S(2)}) collective-permute-start(bf16[1,128,128]{2,1,0:T(8,128)(2,1)S(1)} %get-tuple-element.24), channel_id=1, source_target_pairs={{0,1},{2,3},{4,5},{6,7},{8,9},{10,11},{12,13},{14,15},{16,17},{18,... | collective-permute-start | bytes 98312 | tf_op jit(solution)/shard_map/ppermute | solution.py:16
  50.5 2.6 copy-start.7
  50.5 48.3 %collective-permute-start.1 = (bf16[1,128,128]{2,1,0:T(8,128)(2,1)S(1)}, bf16[1,128,128]{2,1,0:T(8,128)(2,1)S(1)}, u32[]{:S(2)}, u32[]{:S(2)}) collective-permute-start(bf16[1,128,128]{2,1,0:T(8,128)(2,1)S(1)} %get-tuple-element.25), channel_id=1, source_target_pairs={{2,0},{4,2},{6,4},{8,6},{10,8},{12,10},{14,12},{16,14},{18,16},{20... | collective-permute-start | bytes 98312 | tf_op jit(solution)/shard_map/ppermute | solution.py:17
  51.8 47.0 %collective-permute-start.3 = (bf16[1,128,128]{2,1,0:T(8,128)(2,1)S(1)}, bf16[1,128,128]{2,1,0:T(8,128)(2,1)S(1)}, u32[]{:S(2)}, u32[]{:S(2)}) collective-permute-start(bf16[1,128,128]{2,1,0:T(8,128)(2,1)S(1)} %get-tuple-element.26), channel_id=1, source_target_pairs={{1,0},{3,2},{5,4},{7,6},{9,8},{11,10},{13,12},{15,14},{17,16},{19,... | collective-permute-start | bytes 98312 | tf_op jit(solution)/shard_map/ppermute | solution.py:17
  53.3 0.7 copy-start.3
  54.2 41.3 %copy-start.4 = (bf16[1,1,32,1024]{3,2,1,0:T(8,128)(2,1)S(1)}, bf16[1,1,32,1024]{3,2,1,0:T(8,128)(2,1)}, u32[]{:S(2)}) copy-start(bf16[1,1,32,1024]{3,2,1,0:T(8,128)(2,1)} %param.14) | copy-start | bytes 196612
  101.2 6.2 %collective-permute-start.4 = (bf16[1,128,128]{2,1,0:T(8,128)(2,1)S(1)}, bf16[1,128,128]{2,1,0:T(8,128)(2,1)S(1)}, u32[]{:S(2)}, u32[]{:S(2)}) collective-permute-start(bf16[1,128,128]{2,1,0:T(8,128)(2,1)S(1)} %get-tuple-element.19), channel_id=1, source_target_pairs={{0,2},{2,4},{4,6},{6,8},{8,10},{10,12},{12,14},{14,16},{16,18},{18... | collective-permute-start | bytes 98312 | tf_op jit(solution)/shard_map/ppermute | solution.py:16
  102.5 4.9 %collective-permute-start.6 = (bf16[1,128,128]{2,1,0:T(8,128)(2,1)S(1)}, bf16[1,128,128]{2,1,0:T(8,128)(2,1)S(1)}, u32[]{:S(2)}, u32[]{:S(2)}) collective-permute-start(bf16[1,128,128]{2,1,0:T(8,128)(2,1)S(1)} %get-tuple-element.20), channel_id=1, source_target_pairs={{0,1},{2,3},{4,5},{6,7},{8,9},{10,11},{12,13},{14,15},{16,17},{18,... | collective-permute-start | bytes 98312 | tf_op jit(solution)/shard_map/ppermute | solution.py:16
  104.8 5.8 %collective-permute-start.5 = (bf16[1,128,128]{2,1,0:T(8,128)(2,1)S(1)}, bf16[1,128,128]{2,1,0:T(8,128)(2,1)S(1)}, u32[]{:S(2)}, u32[]{:S(2)}) collective-permute-start(bf16[1,128,128]{2,1,0:T(8,128)(2,1)S(1)} %get-tuple-element.21), channel_id=1, source_target_pairs={{2,0},{4,2},{6,4},{8,6},{10,8},{12,10},{14,12},{16,14},{18,16},{20... | collective-permute-start | bytes 98312 | tf_op jit(solution)/shard_map/ppermute | solution.py:17
  106.1 4.5 %collective-permute-start.7 = (bf16[1,128,128]{2,1,0:T(8,128)(2,1)S(1)}, bf16[1,128,128]{2,1,0:T(8,128)(2,1)S(1)}, u32[]{:S(2)}, u32[]{:S(2)}) collective-permute-start(bf16[1,128,128]{2,1,0:T(8,128)(2,1)S(1)} %get-tuple-element.22), channel_id=1, source_target_pairs={{1,0},{3,2},{5,4},{7,6},{9,8},{11,10},{13,12},{15,14},{17,16},{19,... | collective-permute-start | bytes 98312 | tf_op jit(solution)/shard_map/ppermute | solution.py:17
  110.6 0.7 copy-start.5
  111.3 2.4 copy-start.2
  194.5 49.0 %collective-permute-start.8 = (bf16[1,128,128]{2,1,0:T(8,128)(2,1)S(1)}, bf16[1,128,128]{2,1,0:T(8,128)(2,1)S(1)}, u32[]{:S(2)}, u32[]{:S(2)}) collective-permute-start(bf16[1,128,128]{2,1,0:T(8,128)(2,1)S(1)} %get-tuple-element.15), channel_id=1, source_target_pairs={{0,2},{2,4},{4,6},{6,8},{8,10},{10,12},{12,14},{14,16},{16,18},{18... | collective-permute-start | bytes 98312 | tf_op jit(solution)/shard_map/ppermute | solution.py:16
  198.6 44.8 %collective-permute-start.10 = (bf16[1,128,128]{2,1,0:T(8,128)(2,1)S(1)}, bf16[1,128,128]{2,1,0:T(8,128)(2,1)S(1)}, u32[]{:S(2)}, u32[]{:S(2)}) collective-permute-start(bf16[1,128,128]{2,1,0:T(8,128)(2,1)S(1)} %get-tuple-element.16), channel_id=1, source_target_pairs={{0,1},{2,3},{4,5},{6,7},{8,9},{10,11},{12,13},{14,15},{16,17},{18,... | collective-permute-start | bytes 98312 | tf_op jit(solution)/shard_map/ppermute | solution.py:16
  199.9 43.5 %collective-permute-start.9 = (bf16[1,128,128]{2,1,0:T(8,128)(2,1)S(1)}, bf16[1,128,128]{2,1,0:T(8,128)(2,1)S(1)}, u32[]{:S(2)}, u32[]{:S(2)}) collective-permute-start(bf16[1,128,128]{2,1,0:T(8,128)(2,1)S(1)} %get-tuple-element.17), channel_id=1, source_target_pairs={{2,0},{4,2},{6,4},{8,6},{10,8},{12,10},{14,12},{16,14},{18,16},{20... | collective-permute-start | bytes 98312 | tf_op jit(solution)/shard_map/ppermute | solution.py:17
  201.2 42.2 %collective-permute-start.11 = (bf16[1,128,128]{2,1,0:T(8,128)(2,1)S(1)}, bf16[1,128,128]{2,1,0:T(8,128)(2,1)S(1)}, u32[]{:S(2)}, u32[]{:S(2)}) collective-permute-start(bf16[1,128,128]{2,1,0:T(8,128)(2,1)S(1)} %get-tuple-element.18), channel_id=1, source_target_pairs={{1,0},{3,2},{5,4},{7,6},{9,8},{11,10},{13,12},{15,14},{17,16},{19,... | collective-permute-start | bytes 98312 | tf_op jit(solution)/shard_map/ppermute | solution.py:17
  245.8 6.2 %collective-permute-start.12 = (bf16[1,128,128]{2,1,0:T(8,128)(2,1)S(1)}, bf16[1,128,128]{2,1,0:T(8,128)(2,1)S(1)}, u32[]{:S(2)}, u32[]{:S(2)}) collective-permute-start(bf16[1,128,128]{2,1,0:T(8,128)(2,1)S(1)} %get-tuple-element.11), channel_id=1, source_target_pairs={{0,2},{2,4},{4,6},{6,8},{8,10},{10,12},{12,14},{14,16},{16,18},{18... | collective-permute-start | bytes 98312 | tf_op jit(solution)/shard_map/ppermute | solution.py:16
  247.1 4.9 %collective-permute-start.14 = (bf16[1,128,128]{2,1,0:T(8,128)(2,1)S(1)}, bf16[1,128,128]{2,1,0:T(8,128)(2,1)S(1)}, u32[]{:S(2)}, u32[]{:S(2)}) collective-permute-start(bf16[1,128,128]{2,1,0:T(8,128)(2,1)S(1)} %get-tuple-element.12), channel_id=1, source_target_pairs={{0,1},{2,3},{4,5},{6,7},{8,9},{10,11},{12,13},{14,15},{16,17},{18,... | collective-permute-start | bytes 98312 | tf_op jit(solution)/shard_map/ppermute | solution.py:16
  249.3 5.8 %collective-permute-start.13 = (bf16[1,128,128]{2,1,0:T(8,128)(2,1)S(1)}, bf16[1,128,128]{2,1,0:T(8,128)(2,1)S(1)}, u32[]{:S(2)}, u32[]{:S(2)}) collective-permute-start(bf16[1,128,128]{2,1,0:T(8,128)(2,1)S(1)} %get-tuple-element.13), channel_id=1, source_target_pairs={{2,0},{4,2},{6,4},{8,6},{10,8},{12,10},{14,12},{16,14},{18,16},{20... | collective-permute-start | bytes 98312 | tf_op jit(solution)/shard_map/ppermute | solution.py:17
  250.6 4.5 %collective-permute-start.15 = (bf16[1,128,128]{2,1,0:T(8,128)(2,1)S(1)}, bf16[1,128,128]{2,1,0:T(8,128)(2,1)S(1)}, u32[]{:S(2)}, u32[]{:S(2)}) collective-permute-start(bf16[1,128,128]{2,1,0:T(8,128)(2,1)S(1)} %get-tuple-element.14), channel_id=1, source_target_pairs={{1,0},{3,2},{5,4},{7,6},{9,8},{11,10},{13,12},{15,14},{17,16},{19,... | collective-permute-start | bytes 98312 | tf_op jit(solution)/shard_map/ppermute | solution.py:17
where the time goes:
time: 378 us; the launch traced here: 377 us
  blocking collectives  321 us (85%)
  starting transfers between devices  28.4 us (8%)
  local copies, waits for them, and re-layouts  11.2 us (3%)
  other arithmetic  6.8 us (2%)
  waiting for transfers between devices  6.4 us (2%)
    psum x3, blocking collectives, column_norm(): squares = lax.psum(jnp.sum(vector * vector, axis=0), ('gx', 'gy'))  123 us
    psum x3, blocking collectives, project_single(): return lax.psum(jnp.sum(vector * direction, axis=0), ('gx', 'gy'))  116 us
    all_gather x2, blocking collectives, precondition(): lax.all_gather(residual, ('gx', 'gy'), axis=0, tiled=True)  82.1 us
    ppermute x8, starting transfers between devices, padded(): before = lax.ppermute(last, axis, up)  18 us
    ppermute x8, starting transfers between devices, padded(): after = lax.ppermute(initial, axis, down)  10.3 us
  transfers between devices with their start and end apart: 16, of which 2 were waited for; matrix products, arithmetic and copies ran while one was open for 1% of the time, Pallas kernels for 0%

commit v1 on v0

v1 whole, which is shorter than its diff:
```python
import functools

import jax
import jax.numpy as jnp
from jax import lax
from jax.experimental import pallas as pl
from jax.experimental.pallas import tpu as pltpu
from jax.sharding import PartitionSpec as P

EPSILON = 1e-06
MESH = pl.DeviceIdType.MESH
F32 = jnp.float32
BF16 = jnp.bfloat16
LANES = 128


def least_squares(scale_norm, first_dot, first_norm, cross_dot, second_dot, second_norm):
    radius_one = jnp.sqrt(first_dot * first_dot + first_norm * first_norm)
    cosine_one = first_dot / radius_one
    sine_one = first_norm / radius_one
    upper_entry = cosine_one * cross_dot + sine_one * second_dot
    lower_entry = cosine_one * second_dot - sine_one * cross_dot
    radius_two = jnp.sqrt(lower_entry * lower_entry + second_norm * second_norm)
    cosine_two = lower_entry / radius_two
    sine_two = second_norm / radius_two
    weight_two = -cosine_two * sine_one * scale_norm / radius_two
    weight_one = (cosine_one * scale_norm - upper_entry * weight_two) / radius_one
    return (weight_one, weight_two, sine_one * sine_two)


def dot(left, right):
    return jnp.dot(left, right, preferred_element_type=F32)


def repeat(first, last, body):
    if last - first <= 8:
        for index in range(first, last):
            body(index)
    else:
        lax.fori_loop(first, last, lambda index, carry: (body(index), carry)[1], 0)


def column_sum(values):
    return jnp.sum(values, axis=0, keepdims=True)


def kernel(
    n_gx,
    n_gy,
    plane,
    rhs_ref,
    rows_ref,
    weight_ref,
    block_ref,
    inverse_ref,
    basis_ref,
    coarse_ref,
    map_ref,
    out_ref,
    relative_ref,
    coarse_t,
    pieces,
    solver,
    select,
    spread,
    basis_t,
    packs,
    margins,
    gathered,
    partial,
    received,
    line_sums,
    plane_sums,
    pieces_sem,
    margin_send,
    margin_recv,
    gather_sem,
    partial_sem,
    line_sem,
    plane_sem,
):
    i = lax.axis_index("gx")
    j = lax.axis_index("gy")
    n_line = n_gx // plane
    n_plane = plane * n_gy
    line = i // plane
    spot = (i % plane) * n_gy + j
    owned, columns = rhs_ref.shape
    width = basis_ref.shape[1]

    def line_device(slot):
        return (slot * plane + i % plane, j)

    def plane_device(slot):
        return (line * plane + slot // n_gy, slot % n_gy)

    faces = (
        ((i - 1, j), i > 0, 1),
        ((i + 1, j), i < n_gx - 1, 0),
        ((i, j - 1), j > 0, 3),
        ((i, j + 1), j < n_gy - 1, 2),
    )

    for face, (_, present, _) in enumerate(faces):

        @pl.when(jnp.logical_not(present))
        def _():
            for exchange in range(margins.shape[0]):
                margins[exchange, face] = jnp.zeros(margins.shape[2:], BF16)

    barrier = pltpu.get_barrier_semaphore()

    def greet(device):
        pl.semaphore_signal(barrier, inc=1, device_id=device, device_id_type=MESH)

    repeat(1, n_line, lambda step: greet(line_device((line + step) % n_line)))
    repeat(1, n_plane, lambda step: greet(plane_device((spot + step) % n_plane)))
    cross_down = jnp.logical_and(i % plane == 0, i > 0)
    cross_up = jnp.logical_and(i % plane == plane - 1, i < n_gx - 1)
    if plane > 1:

        @pl.when(cross_down)
        def _():
            greet((i - 1, j))

        @pl.when(cross_up)
        def _():
            greet((i + 1, j))

    right_side = rhs_ref[...]
    square_sum = column_sum(right_side * right_side)

    peers = n_line + n_plane - 2
    if plane > 1:
        peers += cross_down.astype(jnp.int32) + cross_up.astype(jnp.int32)
    pl.semaphore_wait(barrier, peers)

    def start_copy(source, target, sends, recvs, device):
        pltpu.make_async_remote_copy(
            src_ref=source,
            dst_ref=target,
            send_sem=sends,
            recv_sem=recvs,
            device_id=device,
            device_id_type=MESH,
        ).start()

    def wait_bytes(ref, sem):
        pltpu.make_async_copy(ref, ref, sem).wait()

    def line_gather(slots, sems):
        def send(step):
            device = line_device((line + step) % n_line)
            start_copy(slots.at[line], slots.at[line], sems.at[0], sems.at[1], device)

        repeat(1, n_line, send)

    def plane_gather(slots, sems):
        def send(step):
            device = plane_device((spot + step) % n_plane)
            start_copy(slots.at[spot], slots.at[spot], sems.at[0], sems.at[1], device)

        repeat(1, n_plane, send)

    def plane_scatter(sources, slots, sems):
        def send(step):
            other = (spot + step) % n_plane
            start_copy(
                sources.at[other], slots.at[spot], sems.at[0], sems.at[1], plane_device(other)
            )

        repeat(1, n_plane, send)

    def wait_line(slots, sems, which):
        if n_line > 1:
            wait_bytes(slots.at[pl.ds(0, n_line - 1)], sems.at[which])

    def wait_plane(slots, sems, which):
        if n_plane > 1:
            wait_bytes(slots.at[pl.ds(0, n_plane - 1)], sems.at[which])

    def start_sums(which, sums):
        rest = jnp.zeros((8 - len(sums), columns), F32)
        line_sums[which, line] = jnp.concatenate(list(sums) + [rest], axis=0)
        line_gather(line_sums.at[which], line_sem.at[which])

    def finish_sums(which, count):
        wait_line(line_sums.at[which], line_sem.at[which], 1)
        plane_sums[which, spot] = jnp.sum(line_sums[which], axis=0)
        plane_gather(plane_sums.at[which], plane_sem.at[which])
        wait_plane(plane_sums.at[which], plane_sem.at[which], 1)
        total = jnp.sum(plane_sums[which], axis=0)
        return [total[row : row + 1, :] for row in range(count)]

    start_sums(0, [square_sum])

    row_ids = lax.broadcasted_iota(jnp.int32, (owned, rows_ref.shape[1]), 0)
    for face in range(4):
        hit = row_ids == rows_ref[face : face + 1, :]
        one = jnp.where(hit, 1.0, 0.0).astype(F32)
        select[face] = one.T.astype(BF16)
        weights = jnp.where(hit, weight_ref[face : face + 1, :], 0.0)
        high = weights.astype(BF16)
        spread[0, face] = high
        spread[1, face] = (weights - high.astype(F32)).astype(BF16)
    basis_t[...] = basis_ref[...].astype(F32).T.astype(BF16)

    [beta_square] = finish_sums(0, 1)
    beta = jnp.sqrt(beta_square + EPSILON)

    def turn(chunk):
        start = chunk * LANES
        if not isinstance(start, int):
            start = pl.multiple_of(start, LANES)
        turned = coarse_ref[:, pl.ds(start, LANES)].astype(F32).T
        count = LANES // width
        coarse_t[pl.ds(chunk * count, count)] = turned.reshape(count, width, width)

    def arrange(member):
        parts = []
        for other_line in range(n_line):
            parts.append(coarse_t[map_ref[other_line * n_plane + member]])
        pieces[member] = jnp.concatenate(parts, axis=0).T.astype(BF16)

    def send_pieces():
        repeat(0, coarse_ref.shape[1] // LANES, turn)
        repeat(0, n_plane, arrange)
        plane_scatter(pieces, solver, pieces_sem)
        solver[spot] = pieces[spot]

    def start_margins(exchange, rounded):
        packs[exchange] = dot(
            select[...].reshape(-1, owned), rounded
        ).astype(BF16).reshape(packs.shape[1:])
        for face, (device, present, block) in enumerate(faces):

            @pl.when(present)
            def _():
                start_copy(
                    packs.at[exchange, face],
                    margins.at[exchange, block],
                    margin_send.at[exchange, face],
                    margin_recv.at[exchange, block],
                    device,
                )

    def wait_margins(exchange):
        for face, (_, present, _) in enumerate(faces):

            @pl.when(present)
            def _():
                wait_bytes(margins.at[exchange, face], margin_recv.at[exchange, face])

    def precondition(turn_index, vector):
        exchange = 2 * turn_index
        rounded = vector.astype(BF16)
        residual = dot(basis_t[...], rounded).astype(BF16)
        gathered[turn_index, line] = residual
        line_gather(gathered.at[turn_index], gather_sem.at[turn_index])
        start_margins(exchange, rounded)
        if turn_index == 0:
            send_pieces()
        local = dot(inverse_ref[:, :owned], rounded)
        if turn_index == 0:
            wait_plane(solver, pieces_sem, 1)
        wait_line(gathered.at[turn_index], gather_sem.at[turn_index], 1)
        partial[turn_index] = dot(
            solver[...].reshape(n_plane * width, n_line * width),
            gathered[turn_index].reshape(n_line * width, columns),
        ).reshape(n_plane, width, columns)
        plane_scatter(
            partial.at[turn_index], received.at[turn_index], partial_sem.at[turn_index]
        )
        received[turn_index, spot] = partial[turn_index, spot]
        wait_margins(exchange)
        local += dot(inverse_ref[:, owned:], margins[exchange].reshape(-1, columns))
        wait_plane(received.at[turn_index], partial_sem.at[turn_index], 1)
        solved = jnp.sum(received[turn_index], axis=0).astype(BF16)
        return local + dot(basis_ref[...], solved)

    def apply_operator(turn_index, vector):
        exchange = 2 * turn_index + 1
        rounded = vector.astype(BF16)
        start_margins(exchange, rounded)
        size = block_ref.shape[1]
        own = [
            dot(block_ref[block], rounded[block * size : (block + 1) * size])
            for block in range(block_ref.shape[0])
        ]
        own = own[0] if len(own) == 1 else jnp.concatenate(own, axis=0)
        wait_margins(exchange)
        for face in range(4):
            margin = margins[exchange, face]
            own -= dot(spread[0, face], margin) + dot(spread[1, face], margin)
        return own

    krylov_one = right_side / beta
    precond_one = precondition(0, krylov_one)
    applied = apply_operator(0, precond_one)
    start_sums(
        1,
        [
            column_sum(applied * krylov_one),
            column_sum(applied * applied),
            column_sum(krylov_one * krylov_one),
        ],
    )
    first_dot, applied_square, one_one = finish_sums(1, 3)
    remainder_square = applied_square + first_dot * first_dot * (one_one - 2.0)
    first_norm = jnp.sqrt(jnp.maximum(remainder_square, 0.0) + EPSILON)
    krylov_two = (applied - first_dot * krylov_one) / first_norm

    precond_two = precondition(1, krylov_two)
    applied = apply_operator(1, precond_two)
    start_sums(
        2,
        [
            column_sum(applied * krylov_one),
            column_sum(applied * krylov_two),
            column_sum(applied * applied),
            column_sum(krylov_one * krylov_two),
            column_sum(krylov_two * krylov_two),
        ],
    )
    cross_dot, second_dot, applied_square, one_two, two_two = finish_sums(2, 5)
    remainder_square = (
        applied_square
        + cross_dot * cross_dot * (one_one - 2.0)
        + second_dot * second_dot * (two_two - 2.0)
        + 2.0 * cross_dot * second_dot * one_two
    )
    second_norm = jnp.sqrt(jnp.maximum(remainder_square, 0.0) + EPSILON)
    weight_one, weight_two, relative = least_squares(
        beta, first_dot, first_norm, cross_dot, second_dot, second_norm
    )
    out_ref[...] = weight_one * precond_one + weight_two * precond_two
    relative_ref[...] = relative

    for which in range(3):
        wait_line(line_sums.at[which], line_sem.at[which], 0)
        wait_plane(plane_sums.at[which], plane_sem.at[which], 0)
    wait_plane(solver, pieces_sem, 0)
    for turn_index in range(2):
        wait_line(gathered.at[turn_index], gather_sem.at[turn_index], 0)
        wait_plane(received.at[turn_index], partial_sem.at[turn_index], 0)
    for exchange in range(4):
        for face, (_, present, _) in enumerate(faces):

            @pl.when(present)
            def _():
                wait_bytes(packs.at[exchange, face], margin_send.at[exchange, face])


def on_device(
    n_gx,
    n_gy,
    rhs,
    face_rows,
    margin_weight,
    local_blocks,
    subdomain_inverse,
    coarse_basis,
    coarse_inverse,
    coarse_map,
):
    plane = 4 if n_gx % 4 == 0 else 1
    n_line, n_plane = n_gx // plane, plane * n_gy
    owned, columns = rhs.shape[2:]
    margin_rows = face_rows.shape[3]
    width = coarse_basis.shape[3]
    n_coarse = coarse_inverse.shape[3]
    vmem = pl.BlockSpec(memory_space=pltpu.VMEM)
    dma = pltpu.SemaphoreType.DMA
    result, relative = pl.pallas_call(
        functools.partial(kernel, n_gx, n_gy, plane),
        out_shape=(
            jax.ShapeDtypeStruct((owned, columns), F32),
            jax.ShapeDtypeStruct((1, columns), F32),
        ),
        in_specs=[vmem] * 7 + [pl.BlockSpec(memory_space=pltpu.SMEM)],
        out_specs=(vmem, vmem),
        scratch_shapes=[
            pltpu.VMEM((n_coarse // width, width, width), F32),
            pltpu.VMEM((n_plane, width, n_line * width), BF16),
            pltpu.VMEM((n_plane, width, n_line * width), BF16),
            pltpu.VMEM((4, margin_rows, owned), BF16),
            pltpu.VMEM((2, 4, owned, margin_rows), BF16),
            pltpu.VMEM((width, owned), BF16),
            pltpu.VMEM((4, 4, margin_rows, columns), BF16),
            pltpu.VMEM((4, 4, margin_rows, columns), BF16),
            pltpu.VMEM((2, n_line, width, columns), BF16),
            pltpu.VMEM((2, n_plane, width, columns), F32),
            pltpu.VMEM((2, n_plane, width, columns), F32),
            pltpu.VMEM((3, n_line, 8, columns), F32),
            pltpu.VMEM((3, n_plane, 8, columns), F32),
            dma((2,)),
            dma((4, 4)),
            dma((4, 4)),
            dma((2, 2)),
            dma((2, 2)),
            dma((3, 2)),
            dma((3, 2)),
        ],
        compiler_params=pltpu.CompilerParams(
            collective_id=0, has_side_effects=True, vmem_limit_bytes=40 * 1024 * 1024
        ),
    )(
        rhs[0, 0],
        face_rows[0, 0],
        margin_weight[0, 0],
        local_blocks[0, 0],
        subdomain_inverse[0, 0],
        coarse_basis[0, 0],
        coarse_inverse[0, 0],
        coarse_map,
    )
    return (result[None, None], relative[0])


def solution(mesh):
    return jax.shard_map(
        functools.partial(on_device, mesh.shape["gx"], mesh.shape["gy"]),
        mesh=mesh,
        in_specs=(
            P("gx", "gy", None, None),
            P("gx", "gy", None, None),
            P("gx", "gy", None, None),
            P("gx", "gy", None, None, None),
            P("gx", "gy", None, None),
            P("gx", "gy", None, None),
            P("gx", "gy", None, None),
            P(),
        ),
        out_specs=(P("gx", "gy", None, None), P()),
        check_vma=False,
    )
```

time: 378 us -> 56.8 us (0.15)
  blocking collectives: 321 us -> 0 us
  Pallas kernels: 0 us -> 50.6 us
  starting transfers between devices: 28.4 us -> 0 us
  other arithmetic: 6.8 us -> 0 us
  waiting for transfers between devices: 6.4 us -> 0 us
  local copies, waits for them, and re-layouts: 11.2 us -> 5.19 us
    psum x6 -> x0, blocking collectives: 239 us -> none  [the longest x3 123 us: column_norm(): squares = lax.psum(jnp.sum(vector * vector, axis=0), ('gx', 'gy'))]
    all_gather x2 -> x0, blocking collectives: 82.1 us -> none  [precondition(): lax.all_gather(residual, ('gx', 'gy'), axis=0, tiled=True)]
    pallas_call x0 -> x1, Pallas kernels: none -> 50.6 us  [on_device(): pl.pallas_call(functools.partial(kernel, n_gx, n_gy, plane), out_shape=(j...]
    ppermute x16 -> x0, starting transfers between devices: 28.4 us -> none  [the longest x8 18 us: padded(): before = lax.ppermute(last, axis, up)]
    gather x5 -> x0, local copies, waits for them, and re-layouts: 8.58 us -> none  [the longest x4 5.37 us: neighbour_margin(): face_packs = rounded[margin_rows]]
    ppermute x16 -> x0, waiting for transfers between devices: 6.4 us -> none  [the longest x8 6.38 us: padded(): after = lax.ppermute(initial, axis, down)]
    scatter-add x2 -> x0, other arithmetic: 4.79 us -> none  [apply_operator(): coupling = jnp.zeros((owned_rows, system_count), jnp.float32).at[margin_r...]
  transfers between devices with their start and end apart: 16 -> 0, of which waited for: 2 -> 0; matrix products, arithmetic and copies ran while one was open for 1% -> 0% of each run, Pallas kernels for 0% -> 0%
where the time goes in v1:
time: 56.8 us; the launch traced here: 56.5 us
  Pallas kernels  50.6 us (89%)
  local copies, waits for them, and re-layouts  5.19 us (9%)
  between operations  0.68 us (1%)
    pallas_call x1, Pallas kernels, on_device(): pl.pallas_call(functools.partial(kernel, n_gx, n_gy, plane), out_shape=(j...  50.6 us
    unnamed x19, local copies, waits for them, and re-layouts  5.19 us

profile of v1, /device:TPU:0, one launch (start us, length us, event | category | flops | bytes accessed | tf_op | source)
XLA Modules:
  0.0 56.5 jit_solution(16683942561799538042)
XLA Ops:
  0.6 0.0 copy-start.7
  0.6 0.0 copy-start.3
  0.7 0.7 %copy-done.7 = bf16[1,1,128,32]{2,3,1,0:T(8,128)(2,1)S(1)} copy-done((bf16[1,1,128,32]{2,3,1,0:T(8,128)(2,1)S(1)}, bf16[1,1,128,32]{2,3,1,0:T(8,128)(2,1)}, u32[]{:S(2)}) %copy-start.7) | copy-done | bytes 8216
  1.3 0.0 copy-start.4
  1.3 0.0 copy-start.5
  1.3 0.1 copy.10
  1.5 0.0 copy-start.6
  1.5 0.0 copy-done.3
  1.5 0.5 copy-done.4
  2.0 0.0 copy-done.5
  2.0 0.1 copy-done.6
  2.1 0.0 copy-start
  2.1 0.9 %copy-done = bf16[1,1,128,640]{3,2,1,0:T(8,128)(2,1)S(1)} copy-done((bf16[1,1,128,640]{3,2,1,0:T(8,128)(2,1)S(1)}, bf16[1,1,128,640]{3,2,1,0:T(8,128)(2,1)}, u32[]{:S(2)}) %copy-start) | copy-done | bytes 163864
  3.0 0.0 copy-start.1
  3.0 0.8 %copy-done.1 = f32[1,1,128,128]{3,2,1,0:T(8,128)S(1)} copy-done((f32[1,1,128,128]{3,2,1,0:T(8,128)S(1)}, f32[1,1,128,128]{3,2,1,0:T(8,128)}, u32[]{:S(2)}) %copy-start.1) | copy-done | bytes 65560
  3.9 0.0 copy-start.2
  3.9 0.8 %copy-done.2 = bf16[1,1,32,1024]{3,2,1,0:T(8,128)(2,1)S(1)} copy-done((bf16[1,1,32,1024]{3,2,1,0:T(8,128)(2,1)S(1)}, bf16[1,1,32,1024]{3,2,1,0:T(8,128)(2,1)}, u32[]{:S(2)}) %copy-start.2) | copy-done | bytes 65560
  4.7 50.6 %shard_map.95 = (f32[128,128]{1,0:T(8,128)S(1)}, f32[1,128]{1,0:T(1,128)S(1)}) custom-call(f32[128,128]{1,0:T(8,128)S(1)} %bitcast.12, s32[4,128]{1,0:T(4,128)S(1)} %bitcast.15, f32[4,128]{1,0:T(4,128)S(1)} %bitcast.16, bf16[1,128,128]{2,1,0:T(8,128)(2,1)S(1)} %bitcast.14, bf16[128,640]{1,0:T(8,128)(2,1)S(1)} %bitcast.9, bf16[128,32]{1,0:T(8,128)(2,1)S(1)} %bitcast.10, ...), custom_call_target="tpu_custom_call" | custom-call | tf_op jit(solution)/shard_map/pallas_call | solution.py:374
  55.4 0.6 %copy.13 = f32[1,1,128,128]{3,2,1,0:T(8,128)} copy(f32[1,1,128,128]{3,2,1,0:T(8,128)S(1)} %bitcast.11) | data formatting | bytes 131072
  56.0 0.5 copy.14
Async XLA Ops:
  0.6 0.7 %copy-start.7 = (bf16[1,1,128,32]{2,3,1,0:T(8,128)(2,1)S(1)}, bf16[1,1,128,32]{2,3,1,0:T(8,128)(2,1)}, u32[]{:S(2)}) copy-start(bf16[1,1,128,32]{2,3,1,0:T(8,128)(2,1)} %param.13) | copy-start | bytes 24580
  0.6 0.8 %copy-start.3 = (bf16[1,1,1,128,128]{4,3,2,1,0:T(8,128)(2,1)S(1)}, bf16[1,1,1,128,128]{4,3,2,1,0:T(8,128)(2,1)}, u32[]{:S(2)}) copy-start(bf16[1,1,1,128,128]{4,3,2,1,0:T(8,128)(2,1)} %param.11) | copy-start | bytes 98308
  1.3 0.7 %copy-start.4 = (s32[1,1,4,128]{3,2,1,0:T(4,128)S(1)}, s32[1,1,4,128]{3,2,1,0:T(4,128)}, u32[]{:S(2)}) copy-start(s32[1,1,4,128]{3,2,1,0:T(4,128)} %param.9) | copy-start | bytes 6148
  1.3 0.7 %copy-start.5 = (f32[1,1,4,128]{3,2,1,0:T(4,128)S(1)}, f32[1,1,4,128]{3,2,1,0:T(4,128)}, u32[]{:S(2)}) copy-start(f32[1,1,4,128]{3,2,1,0:T(4,128)} %param.10) | copy-start | bytes 6148
  1.5 0.7 %copy-start.6 = (s32[32]{0:T(128)S(1)}, s32[32]{0:T(128)}, u32[]{:S(2)}) copy-start(s32[32]{0:T(128)} %map_ref.1) | copy-start | bytes 388
  2.1 0.9 %copy-start = (bf16[1,1,128,640]{3,2,1,0:T(8,128)(2,1)S(1)}, bf16[1,1,128,640]{3,2,1,0:T(8,128)(2,1)}, u32[]{:S(2)}) copy-start(bf16[1,1,128,640]{3,2,1,0:T(8,128)(2,1)} %param.12) | copy-start | bytes 491524
  3.0 0.8 %copy-start.1 = (f32[1,1,128,128]{3,2,1,0:T(8,128)S(1)}, f32[1,1,128,128]{3,2,1,0:T(8,128)}, u32[]{:S(2)}) copy-start(f32[1,1,128,128]{3,2,1,0:T(8,128)} %param.8) | copy-start | bytes 196612
  3.9 0.8 %copy-start.2 = (bf16[1,1,32,1024]{3,2,1,0:T(8,128)(2,1)S(1)}, bf16[1,1,32,1024]{3,2,1,0:T(8,128)(2,1)}, u32[]{:S(2)}) copy-start(bf16[1,1,32,1024]{3,2,1,0:T(8,128)(2,1)} %param.14) | copy-start | bytes 196612

commit v2 on v1

v2 whole, which is shorter than its diff:
```python
import functools

import jax
import jax.numpy as jnp
from jax import lax
from jax.experimental import pallas as pl
from jax.experimental.pallas import tpu as pltpu
from jax.sharding import PartitionSpec as P

EPSILON = 1e-06
MESH = pl.DeviceIdType.MESH
F32 = jnp.float32
BF16 = jnp.bfloat16
LANES = 128


def least_squares(scale_norm, first_dot, first_norm, cross_dot, second_dot, second_norm):
    radius_one = jnp.sqrt(first_dot * first_dot + first_norm * first_norm)
    cosine_one = first_dot / radius_one
    sine_one = first_norm / radius_one
    upper_entry = cosine_one * cross_dot + sine_one * second_dot
    lower_entry = cosine_one * second_dot - sine_one * cross_dot
    radius_two = jnp.sqrt(lower_entry * lower_entry + second_norm * second_norm)
    cosine_two = lower_entry / radius_two
    sine_two = second_norm / radius_two
    weight_two = -cosine_two * sine_one * scale_norm / radius_two
    weight_one = (cosine_one * scale_norm - upper_entry * weight_two) / radius_one
    return (weight_one, weight_two, sine_one * sine_two)


def dot(left, right):
    return jnp.dot(left, right, preferred_element_type=F32)


def repeat(first, last, body):
    if last - first <= 8:
        for index in range(first, last):
            body(index)
    else:
        lax.fori_loop(first, last, lambda index, carry: (body(index), carry)[1], 0)


def column_sum(values):
    return jnp.sum(values, axis=0, keepdims=True)


def halves(values):
    high = values.astype(BF16)
    low = (values - high.astype(F32)).astype(BF16)
    return jnp.concatenate([high, low], axis=1)


def joined(values):
    columns = values.shape[1] // 2
    return values[:, :columns] + values[:, columns:]


def kernel(
    n_gx,
    n_gy,
    plane,
    rhs_hbm,
    rows_hbm,
    weight_hbm,
    block_hbm,
    inverse_hbm,
    basis_t_hbm,
    coarse_hbm,
    map_hbm,
    out_ref,
    relative_ref,
    rhs_ref,
    rows_ref,
    weight_ref,
    block_ref,
    inverse_ref,
    basis_t,
    coarse_ref,
    map_ref,
    coarse_t,
    pieces,
    solver,
    select,
    spread,
    basis_ref,
    packs,
    margins,
    gathered,
    partial,
    received,
    line_sums,
    plane_sums,
    operand_sem,
    pieces_sem,
    margin_send,
    margin_recv,
    gather_sem,
    partial_sem,
    line_sem,
    plane_sem,
):
    i = lax.axis_index("gx")
    j = lax.axis_index("gy")
    n_line = n_gx // plane
    n_plane = plane * n_gy
    line = i // plane
    spot = (i % plane) * n_gy + j
    owned, columns = rhs_ref.shape
    width = basis_ref.shape[1]

    def line_device(slot):
        return (slot * plane + i % plane, j)

    def plane_device(slot):
        return (line * plane + slot // n_gy, slot % n_gy)

    barrier = pltpu.get_barrier_semaphore()

    def greet(device):
        pl.semaphore_signal(barrier, inc=1, device_id=device, device_id_type=MESH)

    repeat(1, n_line, lambda step: greet(line_device((line + step) % n_line)))
    repeat(1, n_plane, lambda step: greet(plane_device((spot + step) % n_plane)))
    cross_down = jnp.logical_and(i % plane == 0, i > 0)
    cross_up = jnp.logical_and(i % plane == plane - 1, i < n_gx - 1)
    peers = n_line + n_plane - 2
    if plane > 1:
        peers += cross_down.astype(jnp.int32) + cross_up.astype(jnp.int32)

        @pl.when(cross_down)
        def _():
            greet((i - 1, j))

        @pl.when(cross_up)
        def _():
            greet((i + 1, j))

    operands = {}
    for index, (name, source, target) in enumerate(
        (
            ("coarse", coarse_hbm, coarse_ref),
            ("map", map_hbm, map_ref),
            ("rhs", rhs_hbm, rhs_ref),
            ("basis", basis_t_hbm, basis_t),
            ("rows", rows_hbm, rows_ref),
            ("weight", weight_hbm, weight_ref),
            ("inverse", inverse_hbm, inverse_ref),
            ("block", block_hbm, block_ref),
        )
    ):
        operands[name] = pltpu.make_async_copy(source, target, operand_sem.at[index])
        operands[name].start()

    faces = (
        ((i - 1, j), i > 0, 1),
        ((i + 1, j), i < n_gx - 1, 0),
        ((i, j - 1), j > 0, 3),
        ((i, j + 1), j < n_gy - 1, 2),
    )

    for face, (_, present, _) in enumerate(faces):

        @pl.when(jnp.logical_not(present))
        def _():
            for exchange in range(margins.shape[0]):
                margins[exchange, face] = jnp.zeros(margins.shape[2:], BF16)

    def start_copy(source, target, sends, recvs, device):
        pltpu.make_async_remote_copy(
            src_ref=source,
            dst_ref=target,
            send_sem=sends,
            recv_sem=recvs,
            device_id=device,
            device_id_type=MESH,
        ).start()

    def wait_bytes(ref, sem):
        pltpu.make_async_copy(ref, ref, sem).wait()

    def line_gather(slots, sems):
        def send(step):
            device = line_device((line + step) % n_line)
            start_copy(slots.at[line], slots.at[line], sems.at[0], sems.at[1], device)

        repeat(1, n_line, send)

    def plane_gather(slots, sems):
        def send(step):
            device = plane_device((spot + step) % n_plane)
            start_copy(slots.at[spot], slots.at[spot], sems.at[0], sems.at[1], device)

        repeat(1, n_plane, send)

    def plane_scatter(sources, slots, sems):
        def send(step):
            other = (spot + step) % n_plane
            start_copy(
                sources.at[other], slots.at[spot], sems.at[0], sems.at[1], plane_device(other)
            )

        repeat(1, n_plane, send)

    def wait_line(slots, sems, which):
        if n_line > 1:
            wait_bytes(slots.at[pl.ds(0, n_line - 1)], sems.at[which])

    def wait_plane(slots, sems, which):
        if n_plane > 1:
            wait_bytes(slots.at[pl.ds(0, n_plane - 1)], sems.at[which])

    def tile_of(sums):
        rest = jnp.zeros((8 - len(sums), columns), F32)
        return jnp.concatenate(list(sums) + [rest], axis=0)

    def turn(chunk):
        start = chunk * LANES
        if not isinstance(start, int):
            start = pl.multiple_of(start, LANES)
        turned = coarse_ref[:, pl.ds(start, LANES)].astype(F32).T
        count = LANES // width
        coarse_t[pl.ds(chunk * count, count)] = turned.reshape(count, width, width)

    def arrange(member):
        parts = []
        for other_line in range(n_line):
            parts.append(coarse_t[map_ref[other_line * n_plane + member]])
        pieces[member] = jnp.concatenate(parts, axis=0).T.astype(BF16)

    def make_packs(exchange, rounded):
        packs[exchange] = (
            dot(select[...].reshape(-1, owned), rounded)
            .astype(BF16)
            .reshape(packs.shape[1:])
        )

    def send_packs(exchange):
        for face, (device, present, block) in enumerate(faces):

            @pl.when(present)
            def _():
                start_copy(
                    packs.at[exchange, face],
                    margins.at[exchange, block],
                    margin_send.at[exchange, face],
                    margin_recv.at[exchange, block],
                    device,
                )

    def wait_margins(exchange):
        for face, (_, present, _) in enumerate(faces):

            @pl.when(present)
            def _():
                wait_bytes(margins.at[exchange, face], margin_recv.at[exchange, face])

    def store_line(which, parts, sums):
        gathered[which, line] = joined(dot(basis_t[...], parts)).astype(BF16)
        line_sums[which, line] = tile_of(sums)

    def send_line(which):
        line_gather(gathered.at[which], gather_sem.at[which])
        line_gather(line_sums.at[which], line_sem.at[which])

    def precondition(which, parts):
        local = joined(dot(inverse_ref[:, :owned], parts))
        wait_line(gathered.at[which], gather_sem.at[which], 1)
        products = dot(
            solver[...].reshape(n_plane * width, n_line * width),
            gathered[which].reshape(n_line * width, columns),
        ).reshape(n_plane, width, columns)
        partial[which, :, :width, :] = products
        wait_line(line_sums.at[which], line_sem.at[which], 1)
        line_total = jnp.sum(line_sums[which], axis=0)
        for member in range(n_plane):
            partial[which, member, width:, :] = line_total
        plane_scatter(partial.at[which], received.at[which], partial_sem.at[which])
        received[which, spot] = partial[which, spot]
        wait_margins(2 * which)
        local += dot(inverse_ref[:, owned:], margins[2 * which].reshape(-1, columns))
        wait_plane(received.at[which], partial_sem.at[which], 1)
        total = jnp.sum(received[which], axis=0)
        applied = local + joined(dot(basis_ref[...], halves(total[:width])))
        return applied, total[width:]

    def apply_operator(which, vector):
        exchange = 2 * which + 1
        make_packs(exchange, vector.astype(BF16))
        send_packs(exchange)
        parts = halves(vector)
        size = block_ref.shape[1]
        own = [
            joined(dot(block_ref[block], parts[block * size : (block + 1) * size]))
            for block in range(block_ref.shape[0])
        ]
        own = own[0] if len(own) == 1 else jnp.concatenate(own, axis=0)
        wait_margins(exchange)
        for face in range(4):
            margin = margins[exchange, face]
            own -= dot(spread[0, face], margin) + dot(spread[1, face], margin)
        return own

    operands["coarse"].wait()
    operands["map"].wait()
    repeat(0, coarse_ref.shape[1] // LANES, turn)
    repeat(0, n_plane, arrange)
    operands["rhs"].wait()
    operands["basis"].wait()
    right_side = rhs_ref[...]
    basis_ref[...] = basis_t[...].astype(F32).T.astype(BF16)
    parts = halves(right_side)
    store_line(0, parts, [column_sum(right_side * right_side)])
    operands["rows"].wait()
    operands["weight"].wait()
    row_ids = lax.broadcasted_iota(jnp.int32, (owned, rows_ref.shape[1]), 0)
    for face in range(4):
        hit = row_ids == rows_ref[face : face + 1, :]
        select[face] = jnp.where(hit, 1.0, 0.0).astype(F32).T.astype(BF16)
        weights = jnp.where(hit, weight_ref[face : face + 1, :], 0.0)
        high = weights.astype(BF16)
        spread[0, face] = high
        spread[1, face] = (weights - high.astype(F32)).astype(BF16)
    make_packs(0, right_side.astype(BF16))

    pl.semaphore_wait(barrier, peers)
    plane_scatter(pieces, solver, pieces_sem)
    send_line(0)
    send_packs(0)
    solver[spot] = pieces[spot]
    operands["inverse"].wait()
    operands["block"].wait()
    wait_plane(solver, pieces_sem, 1)

    applied, sums = precondition(0, parts)
    rhs_square = sums[0:1]
    beta = jnp.sqrt(rhs_square + EPSILON)
    one_one = rhs_square / (rhs_square + EPSILON)
    krylov_one = right_side / beta
    precond_one = applied / beta

    image = apply_operator(0, precond_one)
    parts = halves(image)
    store_line(1, parts, [column_sum(image * krylov_one), column_sum(image * image)])
    send_line(1)
    make_packs(2, image.astype(BF16))
    send_packs(2)
    applied, sums = precondition(1, parts)
    first_dot, image_square = sums[0:1], sums[1:2]
    remainder_square = image_square + first_dot * first_dot * (one_one - 2.0)
    remainder_square = jnp.maximum(remainder_square, 0.0)
    first_norm = jnp.sqrt(remainder_square + EPSILON)
    precond_two = (applied - first_dot * precond_one) / first_norm

    krylov_two = (image - first_dot * krylov_one) / first_norm
    one_two = first_dot * (1.0 - one_one) / first_norm
    two_two = remainder_square / (remainder_square + EPSILON)
    image = apply_operator(1, precond_two)
    line_sums[2, line] = tile_of(
        [
            column_sum(image * krylov_one),
            column_sum(image * krylov_two),
            column_sum(image * image),
        ]
    )
    line_gather(line_sums.at[2], line_sem.at[2])
    wait_line(line_sums.at[2], line_sem.at[2], 1)
    plane_sums[spot] = jnp.sum(line_sums[2], axis=0)
    plane_gather(plane_sums, plane_sem)
    wait_plane(plane_sums, plane_sem, 1)
    sums = jnp.sum(plane_sums[...], axis=0)
    cross_dot, second_dot, image_square = sums[0:1], sums[1:2], sums[2:3]
    remainder_square = (
        image_square
        + cross_dot * cross_dot * (one_one - 2.0)
        + second_dot * second_dot * (two_two - 2.0)
        + 2.0 * cross_dot * second_dot * one_two
    )
    second_norm = jnp.sqrt(jnp.maximum(remainder_square, 0.0) + EPSILON)
    weight_one, weight_two, relative = least_squares(
        beta, first_dot, first_norm, cross_dot, second_dot, second_norm
    )
    out_ref[...] = weight_one * precond_one + weight_two * precond_two
    relative_ref[...] = relative

    for which in range(3):
        wait_line(line_sums.at[which], line_sem.at[which], 0)
    wait_plane(plane_sums, plane_sem, 0)
    wait_plane(solver, pieces_sem, 0)
    for which in range(2):
        wait_line(gathered.at[which], gather_sem.at[which], 0)
        wait_plane(received.at[which], partial_sem.at[which], 0)
    for exchange in range(4):
        for face, (_, present, _) in enumerate(faces):

            @pl.when(present)
            def _():
                wait_bytes(packs.at[exchange, face], margin_send.at[exchange, face])


def on_device(
    n_gx,
    n_gy,
    rhs,
    face_rows,
    margin_weight,
    local_blocks,
    subdomain_inverse,
    coarse_basis,
    coarse_inverse,
    coarse_map,
):
    plane = 4 if n_gx % 4 == 0 else 1
    n_line, n_plane = n_gx // plane, plane * n_gy
    owned, columns = rhs.shape[2:]
    margin_rows = face_rows.shape[3]
    width = coarse_basis.shape[3]
    n_coarse = coarse_inverse.shape[3]
    vmem = pl.BlockSpec(memory_space=pltpu.VMEM)
    operands = (
        rhs[0, 0],
        face_rows[0, 0],
        margin_weight[0, 0],
        local_blocks[0, 0],
        subdomain_inverse[0, 0],
        coarse_basis[0, 0].T,
        coarse_inverse[0, 0],
        coarse_map,
    )
    dma = pltpu.SemaphoreType.DMA
    result, relative = pl.pallas_call(
        functools.partial(kernel, n_gx, n_gy, plane),
        out_shape=(
            jax.ShapeDtypeStruct((owned, columns), F32),
            jax.ShapeDtypeStruct((1, columns), F32),
        ),
        in_specs=[pl.BlockSpec(memory_space=pl.ANY)] * len(operands),
        out_specs=(vmem, vmem),
        scratch_shapes=[pltpu.VMEM(each.shape, each.dtype) for each in operands[:-1]]
        + [
            pltpu.SMEM(coarse_map.shape, coarse_map.dtype),
            pltpu.VMEM((n_coarse // width, width, width), F32),
            pltpu.VMEM((n_plane, width, n_line * width), BF16),
            pltpu.VMEM((n_plane, width, n_line * width), BF16),
            pltpu.VMEM((4, margin_rows, owned), BF16),
            pltpu.VMEM((2, 4, owned, margin_rows), BF16),
            pltpu.VMEM((owned, width), BF16),
            pltpu.VMEM((4, 4, margin_rows, columns), BF16),
            pltpu.VMEM((4, 4, margin_rows, columns), BF16),
            pltpu.VMEM((2, n_line, width, columns), BF16),
            pltpu.VMEM((2, n_plane, width + 8, columns), F32),
            pltpu.VMEM((2, n_plane, width + 8, columns), F32),
            pltpu.VMEM((3, n_line, 8, columns), F32),
            pltpu.VMEM((n_plane, 8, columns), F32),
            dma((len(operands),)),
            dma((2,)),
            dma((4, 4)),
            dma((4, 4)),
            dma((2, 2)),
            dma((2, 2)),
            dma((3, 2)),
            dma((2,)),
        ],
        compiler_params=pltpu.CompilerParams(
            collective_id=0, has_side_effects=True, vmem_limit_bytes=56 * 1024 * 1024
        ),
    )(*operands)
    return (result[None, None], relative[0])


def solution(mesh):
    return jax.shard_map(
        functools.partial(on_device, mesh.shape["gx"], mesh.shape["gy"]),
        mesh=mesh,
        in_specs=(
            P("gx", "gy", None, None),
            P("gx", "gy", None, None),
            P("gx", "gy", None, None),
            P("gx", "gy", None, None, None),
            P("gx", "gy", None, None),
            P("gx", "gy", None, None),
            P("gx", "gy", None, None),
            P(),
        ),
        out_specs=(P("gx", "gy", None, None), P()),
        check_vma=False,
    )
```

time: 56.8 us -> 39.9 us (0.70)
  Pallas kernels: 50.6 us -> 37.1 us
  local copies, waits for them, and re-layouts: 5.19 us -> 1.99 us
    pallas_call x1, Pallas kernels: 50.6 us -> 37.1 us  [on_device(): pl.pallas_call(functools.partial(kernel, n_gx, n_gy, plane), out_shape=(j...]
    unnamed x19 -> x4, local copies, waits for them, and re-layouts: 5.19 us -> 1.99 us
where the time goes in v2:
time: 39.9 us; the launch traced here: 39.7 us
  Pallas kernels  37.1 us (93%)
  local copies, waits for them, and re-layouts  1.99 us (5%)
  between operations  0.65 us (2%)
    pallas_call x1, Pallas kernels, on_device(): pl.pallas_call(functools.partial(kernel, n_gx, n_gy, plane), out_shape=(j...  37.1 us
    unnamed x4, local copies, waits for them, and re-layouts  1.99 us

profile of v2, /device:TPU:0, one launch (start us, length us, event | category | flops | bytes accessed | tf_op | source)
XLA Modules:
  0.0 39.7 jit_solution(240500044532483100)
XLA Ops:
  0.6 37.1 %shard_map.95 = (f32[128,128]{1,0:T(8,128)}, f32[1,128]{1,0:T(1,128)}) custom-call(f32[128,128]{1,0:T(8,128)} %bitcast.13, s32[4,128]{1,0:T(4,128)} %bitcast.17, f32[4,128]{1,0:T(4,128)} %bitcast.18, bf16[1,128,128]{2,1,0:T(8,128)(2,1)} %bitcast.15, bf16[128,640]{1,0:T(8,128)(2,1)} %bitcast.11, bf16[32,128]{1,0:T(8,128)(2,1)} %bitcast.16, ...), custom_call_target="tpu_custom_call" | custom-call | tf_op jit(solution)/shard_map/pallas_call | solution.py:430
  37.7 0.0 copy-start
  37.7 1.5 %copy.12 = f32[1,1,128,128]{3,2,1,0:T(8,128)} copy(f32[1,1,128,128]{3,2,1,0:T(8,128)} %bitcast.12) | data formatting | bytes 131072
  39.2 0.0 copy-done
  39.2 0.5 %copy.13 = f32[128]{0:T(128)} copy(f32[128]{0:T(128)S(1)} %bitcast.19) | data formatting | bytes 1024
Async XLA Ops:
  37.7 1.5 %copy-start = (f32[1,128]{1,0:T(1,128)S(1)}, f32[1,128]{1,0:T(1,128)}, u32[]{:S(2)}) copy-start(f32[1,128]{1,0:T(1,128)} %get-tuple-element.5) | copy-start | bytes 1540

commit v3 on v2

--- a/solution.py
+++ b/solution.py
@@ -67,8 +67,9 @@
     basis_t_hbm,
     coarse_hbm,
     map_hbm,
-    out_ref,
-    relative_ref,
+    one_hbm,
+    two_hbm,
+    weights_ref,
     rhs_ref,
     rows_ref,
     weight_ref,
@@ -90,7 +91,9 @@
     received,
     line_sums,
     plane_sums,
+    results,
     operand_sem,
+    result_sem,
     pieces_sem,
     margin_send,
     margin_recv,
@@ -337,6 +340,9 @@
     one_one = rhs_square / (rhs_square + EPSILON)
     krylov_one = right_side / beta
     precond_one = applied / beta
+    results[0] = precond_one
+    first_result = pltpu.make_async_copy(results.at[0], one_hbm, result_sem.at[0])
+    first_result.start()
 
     image = apply_operator(0, precond_one)
     parts = halves(image)
@@ -350,6 +356,9 @@
     remainder_square = jnp.maximum(remainder_square, 0.0)
     first_norm = jnp.sqrt(remainder_square + EPSILON)
     precond_two = (applied - first_dot * precond_one) / first_norm
+    results[1] = precond_two
+    second_result = pltpu.make_async_copy(results.at[1], two_hbm, result_sem.at[1])
+    second_result.start()
 
     krylov_two = (image - first_dot * krylov_one) / first_norm
     one_two = first_dot * (1.0 - one_one) / first_norm
@@ -379,8 +388,9 @@
     weight_one, weight_two, relative = least_squares(
         beta, first_dot, first_norm, cross_dot, second_dot, second_norm
     )
-    out_ref[...] = weight_one * precond_one + weight_two * precond_two
-    relative_ref[...] = relative
+    weights_ref[...] = tile_of([weight_one, weight_two, relative])
+    first_result.wait()
+    second_result.wait()
 
     for which in range(3):
         wait_line(line_sums.at[which], line_sem.at[which], 0)
@@ -416,6 +426,7 @@
     width = coarse_basis.shape[3]
     n_coarse = coarse_inverse.shape[3]
     vmem = pl.BlockSpec(memory_space=pltpu.VMEM)
+    hbm = pl.BlockSpec(memory_space=pl.ANY)
     operands = (
         rhs[0, 0],
         face_rows[0, 0],
@@ -427,14 +438,15 @@
         coarse_map,
     )
     dma = pltpu.SemaphoreType.DMA
-    result, relative = pl.pallas_call(
+    one, two, weights = pl.pallas_call(
         functools.partial(kernel, n_gx, n_gy, plane),
         out_shape=(
             jax.ShapeDtypeStruct((owned, columns), F32),
-            jax.ShapeDtypeStruct((1, columns), F32),
+            jax.ShapeDtypeStruct((owned, columns), F32),
+            jax.ShapeDtypeStruct((8, columns), F32),
         ),
-        in_specs=[pl.BlockSpec(memory_space=pl.ANY)] * len(operands),
-        out_specs=(vmem, vmem),
+        in_specs=[hbm] * len(operands),
+        out_specs=(hbm, hbm, vmem),
         scratch_shapes=[pltpu.VMEM(each.shape, each.dtype) for each in operands[:-1]]
         + [
             pltpu.SMEM(coarse_map.shape, coarse_map.dtype),
@@ -451,7 +463,9 @@
             pltpu.VMEM((2, n_plane, width + 8, columns), F32),
             pltpu.VMEM((3, n_line, 8, columns), F32),
             pltpu.VMEM((n_plane, 8, columns), F32),
+            pltpu.VMEM((2, owned, columns), F32),
             dma((len(operands),)),
+            dma((2,)),
             dma((2,)),
             dma((4, 4)),
             dma((4, 4)),
@@ -464,7 +478,8 @@
             collective_id=0, has_side_effects=True, vmem_limit_bytes=56 * 1024 * 1024
         ),
     )(*operands)
-    return (result[None, None], relative[0])
+    result = weights[0:1] * one + weights[1:2] * two
+    return (result[None, None], weights[2])
 
 
 def solution(mesh):

time: 39.9 us -> 40.7 us (1.020)
  other arithmetic: 0 us -> 1.51 us
  local copies, waits for them, and re-layouts: 1.99 us -> 1.3 us
    unnamed x4 -> x0, local copies, waits for them, and re-layouts: 1.99 us -> none
    broadcast_in_dim x0 -> x1, other arithmetic: none -> 1.51 us  [on_device(): return (result[None, None], weights[2])]
    squeeze x0 -> x1, local copies, waits for them, and re-layouts: none -> 1.3 us  [on_device(): return (result[None, None], weights[2])]
where the time goes in v3:
time: 40.7 us; the launch traced here: 40.5 us
  Pallas kernels  37.1 us (91%)
  other arithmetic  1.51 us (4%)
  local copies, waits for them, and re-layouts  1.3 us (3%)
  between operations  0.64 us (2%)
    pallas_call x1, Pallas kernels, on_device(): pl.pallas_call(functools.partial(kernel, n_gx, n_gy, plane), out_shape=(j...  37.1 us
    broadcast_in_dim x1, other arithmetic, on_device(): return (result[None, None], weights[2])  1.51 us
    squeeze x1, local copies, waits for them, and re-layouts, on_device(): return (result[None, None], weights[2])  1.3 us

profile of v3, /device:TPU:0, one launch (start us, length us, event | category | flops | bytes accessed | tf_op | source)
XLA Modules:
  0.0 40.5 jit_solution(9004996774017202950)
XLA Ops:
  0.6 37.1 %shard_map.95 = (f32[128,128]{1,0:T(8,128)}, f32[128,128]{1,0:T(8,128)}, f32[8,128]{1,0:T(8,128)}) custom-call(f32[128,128]{1,0:T(8,128)} %bitcast.18, s32[4,128]{1,0:T(4,128)} %bitcast.22, f32[4,128]{1,0:T(4,128)} %bitcast.23, bf16[1,128,128]{2,1,0:T(8,128)(2,1)} %bitcast.20, bf16[128,640]{1,0:T(8,128)(2,1)} %bitcast.17, bf16[32,128]{1,0:T(8,128)(2,1)} %bitcast.21, ...), custom_call_target="tpu_custom_call" | custom-call | tf_op jit(solution)/shard_map/pallas_call | solution.py:441
  37.7 1.3 %slice_bitcast_fusion = (f32[128]{0:T(128)}, f32[128]{0:T(128)S(1)}, f32[128]{0:T(128)S(1)}) fusion(f32[8,128]{1,0:T(8,128)} %get-tuple-element.5), kind=kLoop, calls=%fused_computation.1 | loop fusion | bytes 3072 | tf_op jit(solution)/shard_map/squeeze | solution.py:482
  39.0 1.5 %add_bitcast_fusion = f32[1,1,128,128]{3,2,1,0:T(8,128)} fusion(f32[128,128]{1,0:T(8,128)} %get-tuple-element.7, f32[128,128]{1,0:T(8,128)} %get-tuple-element.6, f32[128]{0:T(128)S(1)} %get-tuple-element.9, f32[128]{0:T(128)S(1)} %get-tuple-element.10), kind=kLoop, calls=%fused_computation | loop fusion | flops 49152 | bytes 197632 | tf_op jit(solution)/shard_map/broadcast_in_dim | solution.py:482

commit v4 on v2

--- a/solution.py
+++ b/solution.py
@@ -90,7 +90,16 @@
     received,
     line_sums,
     plane_sums,
+    basis_packs,
+    basis_margins,
+    fold,
+    solved,
+    solved_margins,
     operand_sem,
+    basis_send,
+    basis_recv,
+    solved_send,
+    solved_recv,
     pieces_sem,
     margin_send,
     margin_recv,
@@ -164,6 +173,9 @@
         def _():
             for exchange in range(margins.shape[0]):
                 margins[exchange, face] = jnp.zeros(margins.shape[2:], BF16)
+            for which in range(solved_margins.shape[0]):
+                solved_margins[which, face] = jnp.zeros(solved_margins.shape[2:], BF16)
+            basis_margins[face] = jnp.zeros(basis_margins.shape[1:], BF16)
 
     def start_copy(source, target, sends, recvs, device):
         pltpu.make_async_remote_copy(
@@ -234,25 +246,32 @@
             .reshape(packs.shape[1:])
         )
 
-    def send_packs(exchange):
+    def send_faces(sources, targets, sends, recvs):
         for face, (device, present, block) in enumerate(faces):
 
             @pl.when(present)
             def _():
                 start_copy(
-                    packs.at[exchange, face],
-                    margins.at[exchange, block],
-                    margin_send.at[exchange, face],
-                    margin_recv.at[exchange, block],
-                    device,
+                    sources[face], targets.at[block], sends.at[face], recvs.at[block], device
                 )
 
-    def wait_margins(exchange):
+    def wait_faces(targets, sems):
         for face, (_, present, _) in enumerate(faces):
 
             @pl.when(present)
             def _():
-                wait_bytes(margins.at[exchange, face], margin_recv.at[exchange, face])
+                wait_bytes(targets.at[face], sems.at[face])
+
+    def send_packs(exchange):
+        send_faces(
+            [packs.at[exchange, face] for face in range(4)],
+            margins.at[exchange],
+            margin_send.at[exchange],
+            margin_recv.at[exchange],
+        )
+
+    def wait_margins(exchange):
+        wait_faces(margins.at[exchange], margin_recv.at[exchange])
 
     def store_line(which, parts, sums):
         gathered[which, line] = joined(dot(basis_t[...], parts)).astype(BF16)
@@ -262,7 +281,24 @@
         line_gather(gathered.at[which], gather_sem.at[which])
         line_gather(line_sums.at[which], line_sem.at[which])
 
-    def precondition(which, parts):
+    def fold_basis():
+        wait_faces(basis_margins, basis_recv)
+        folds = []
+        for face in range(4):
+            folds.append(
+                sum(
+                    lax.dot_general(
+                        spread[part, face],
+                        basis_margins[face],
+                        (((1,), (1,)), ((), ())),
+                        preferred_element_type=F32,
+                    )
+                    for part in range(2)
+                )
+            )
+        fold[...] = halves(jnp.concatenate(folds, axis=1))
+
+    def apply_both(which, parts):
         local = joined(dot(inverse_ref[:, :owned], parts))
         wait_line(gathered.at[which], gather_sem.at[which], 1)
         products = dot(
@@ -278,27 +314,35 @@
         received[which, spot] = partial[which, spot]
         wait_margins(2 * which)
         local += dot(inverse_ref[:, owned:], margins[2 * which].reshape(-1, columns))
+        make_packs(2 * which + 1, local.astype(BF16))
+        send_packs(2 * which + 1)
+        if which == 0:
+            fold_basis()
         wait_plane(received.at[which], partial_sem.at[which], 1)
         total = jnp.sum(received[which], axis=0)
+        solved[which] = total[:width].astype(BF16)
+        send_faces(
+            [solved.at[which]] * 4,
+            solved_margins.at[which],
+            solved_send.at[which],
+            solved_recv.at[which],
+        )
         applied = local + joined(dot(basis_ref[...], halves(total[:width])))
-        return applied, total[width:]
-
-    def apply_operator(which, vector):
-        exchange = 2 * which + 1
-        make_packs(exchange, vector.astype(BF16))
-        send_packs(exchange)
-        parts = halves(vector)
+        halved = halves(applied)
         size = block_ref.shape[1]
         own = [
-            joined(dot(block_ref[block], parts[block * size : (block + 1) * size]))
+            joined(dot(block_ref[block], halved[block * size : (block + 1) * size]))
             for block in range(block_ref.shape[0])
         ]
         own = own[0] if len(own) == 1 else jnp.concatenate(own, axis=0)
-        wait_margins(exchange)
+        wait_margins(2 * which + 1)
         for face in range(4):
-            margin = margins[exchange, face]
+            margin = margins[2 * which + 1, face]
             own -= dot(spread[0, face], margin) + dot(spread[1, face], margin)
-        return own
+        wait_faces(solved_margins.at[which], solved_recv.at[which])
+        coarse = solved_margins[which].reshape(4 * width, columns)
+        own -= dot(fold[...], jnp.concatenate([coarse, coarse], axis=0))
+        return applied, own, total[width:]
 
     operands["coarse"].wait()
     operands["map"].wait()
@@ -315,7 +359,9 @@
     row_ids = lax.broadcasted_iota(jnp.int32, (owned, rows_ref.shape[1]), 0)
     for face in range(4):
         hit = row_ids == rows_ref[face : face + 1, :]
-        select[face] = jnp.where(hit, 1.0, 0.0).astype(F32).T.astype(BF16)
+        one_hot = jnp.where(hit, 1.0, 0.0).astype(F32)
+        select[face] = one_hot.T.astype(BF16)
+        basis_packs[face] = dot(basis_t[...], one_hot.astype(BF16)).astype(BF16)
         weights = jnp.where(hit, weight_ref[face : face + 1, :], 0.0)
         high = weights.astype(BF16)
         spread[0, face] = high
@@ -326,35 +372,40 @@
     plane_scatter(pieces, solver, pieces_sem)
     send_line(0)
     send_packs(0)
+    send_faces(
+        [basis_packs.at[face] for face in range(4)], basis_margins, basis_send, basis_recv
+    )
     solver[spot] = pieces[spot]
     operands["inverse"].wait()
     operands["block"].wait()
     wait_plane(solver, pieces_sem, 1)
 
-    applied, sums = precondition(0, parts)
+    applied, image, sums = apply_both(0, parts)
     rhs_square = sums[0:1]
     beta = jnp.sqrt(rhs_square + EPSILON)
     one_one = rhs_square / (rhs_square + EPSILON)
     krylov_one = right_side / beta
+    image_one = image / beta
+
+    parts = halves(image_one)
+    store_line(
+        1, parts, [column_sum(image_one * krylov_one), column_sum(image_one * image_one)]
+    )
+    send_line(1)
+    make_packs(2, image_one.astype(BF16))
+    send_packs(2)
     precond_one = applied / beta
-
-    image = apply_operator(0, precond_one)
-    parts = halves(image)
-    store_line(1, parts, [column_sum(image * krylov_one), column_sum(image * image)])
-    send_line(1)
-    make_packs(2, image.astype(BF16))
-    send_packs(2)
-    applied, sums = precondition(1, parts)
+    applied, image, sums = apply_both(1, parts)
     first_dot, image_square = sums[0:1], sums[1:2]
     remainder_square = image_square + first_dot * first_dot * (one_one - 2.0)
     remainder_square = jnp.maximum(remainder_square, 0.0)
     first_norm = jnp.sqrt(remainder_square + EPSILON)
     precond_two = (applied - first_dot * precond_one) / first_norm
 
-    krylov_two = (image - first_dot * krylov_one) / first_norm
+    krylov_two = (image_one - first_dot * krylov_one) / first_norm
     one_two = first_dot * (1.0 - one_one) / first_norm
     two_two = remainder_square / (remainder_square + EPSILON)
-    image = apply_operator(1, precond_two)
+    image = (image - first_dot * image_one) / first_norm
     line_sums[2, line] = tile_of(
         [
             column_sum(image * krylov_one),
@@ -395,6 +446,10 @@
             @pl.when(present)
             def _():
                 wait_bytes(packs.at[exchange, face], margin_send.at[exchange, face])
+
+    wait_faces(basis_packs, basis_send)
+    for which in range(2):
+        wait_faces(solved_margins.at[which], solved_send.at[which])
 
 
 def on_device(
@@ -451,7 +506,16 @@
             pltpu.VMEM((2, n_plane, width + 8, columns), F32),
             pltpu.VMEM((3, n_line, 8, columns), F32),
             pltpu.VMEM((n_plane, 8, columns), F32),
+            pltpu.VMEM((4, width, margin_rows), BF16),
+            pltpu.VMEM((4, width, margin_rows), BF16),
+            pltpu.VMEM((owned, 8 * width), BF16),
+            pltpu.VMEM((2, width, columns), BF16),
+            pltpu.VMEM((2, 4, width, columns), BF16),
             dma((len(operands),)),
+            dma((4,)),
+            dma((4,)),
+            dma((2, 4)),
+            dma((2, 4)),
             dma((2,)),
             dma((4, 4)),
             dma((4, 4)),

time: 39.9 us -> 38.5 us (0.965)
  Pallas kernels: 37.1 us -> 35.7 us
    pallas_call x1, Pallas kernels: 37.1 us -> 35.7 us  [on_device(): pl.pallas_call(functools.partial(kernel, n_gx, n_gy, plane), out_shape=(j...]
where the time goes in v4:
time: 38.5 us; the launch traced here: 38.4 us
  Pallas kernels  35.7 us (93%)
  local copies, waits for them, and re-layouts  1.99 us (5%)
  between operations  0.65 us (2%)
    pallas_call x1, Pallas kernels, on_device(): pl.pallas_call(functools.partial(kernel, n_gx, n_gy, plane), out_shape=(j...  35.7 us
    unnamed x4, local copies, waits for them, and re-layouts  1.99 us

profile of v4, /device:TPU:0, one launch (start us, length us, event | category | flops | bytes accessed | tf_op | source)
XLA Modules:
  0.0 38.4 jit_solution(10835094315861271619)
XLA Ops:
  0.6 35.7 %shard_map.95 = (f32[128,128]{1,0:T(8,128)}, f32[1,128]{1,0:T(1,128)}) custom-call(f32[128,128]{1,0:T(8,128)} %bitcast.13, s32[4,128]{1,0:T(4,128)} %bitcast.17, f32[4,128]{1,0:T(4,128)} %bitcast.18, bf16[1,128,128]{2,1,0:T(8,128)(2,1)} %bitcast.15, bf16[128,640]{1,0:T(8,128)(2,1)} %bitcast.11, bf16[32,128]{1,0:T(8,128)(2,1)} %bitcast.16, ...), custom_call_target="tpu_custom_call" | custom-call | tf_op jit(solution)/shard_map/pallas_call | solution.py:485
  36.4 0.0 copy-start
  36.4 1.5 %copy.12 = f32[1,1,128,128]{3,2,1,0:T(8,128)} copy(f32[1,1,128,128]{3,2,1,0:T(8,128)} %bitcast.12) | data formatting | bytes 131072
  37.9 0.0 copy-done
  37.9 0.5 %copy.13 = f32[128]{0:T(128)} copy(f32[128]{0:T(128)S(1)} %bitcast.19) | data formatting | bytes 1024
Async XLA Ops:
  36.4 1.5 %copy-start = (f32[1,128]{1,0:T(1,128)S(1)}, f32[1,128]{1,0:T(1,128)}, u32[]{:S(2)}) copy-start(f32[1,128]{1,0:T(1,128)} %get-tuple-element.5) | copy-start | bytes 1540

commit v5 on v4

--- a/solution.py
+++ b/solution.py
@@ -32,8 +32,8 @@
     return jnp.dot(left, right, preferred_element_type=F32)
 
 
-def repeat(first, last, body):
-    if last - first <= 8:
+def repeat(first, last, body, unrolled=8):
+    if last - first <= unrolled:
         for index in range(first, last):
             body(index)
     else:
@@ -89,7 +89,7 @@
     partial,
     received,
     line_sums,
-    plane_sums,
+    all_sums,
     basis_packs,
     basis_margins,
     fold,
@@ -106,7 +106,7 @@
     gather_sem,
     partial_sem,
     line_sem,
-    plane_sem,
+    all_sem,
 ):
     i = lax.axis_index("gx")
     j = lax.axis_index("gy")
@@ -128,21 +128,14 @@
     def greet(device):
         pl.semaphore_signal(barrier, inc=1, device_id=device, device_id_type=MESH)
 
-    repeat(1, n_line, lambda step: greet(line_device((line + step) % n_line)))
-    repeat(1, n_plane, lambda step: greet(plane_device((spot + step) % n_plane)))
-    cross_down = jnp.logical_and(i % plane == 0, i > 0)
-    cross_up = jnp.logical_and(i % plane == plane - 1, i < n_gx - 1)
-    peers = n_line + n_plane - 2
-    if plane > 1:
-        peers += cross_down.astype(jnp.int32) + cross_up.astype(jnp.int32)
-
-        @pl.when(cross_down)
-        def _():
-            greet((i - 1, j))
-
-        @pl.when(cross_up)
-        def _():
-            greet((i + 1, j))
+    n_all = n_gx * n_gy
+    place = i * n_gy + j
+
+    def other_device(step):
+        other = (place + step) % n_all
+        return (other // n_gy, other % n_gy)
+
+    lax.fori_loop(1, n_all, lambda step, carry: (greet(other_device(step)), carry)[1], 0)
 
     operands = {}
     for index, (name, source, target) in enumerate(
@@ -197,13 +190,6 @@
 
         repeat(1, n_line, send)
 
-    def plane_gather(slots, sems):
-        def send(step):
-            device = plane_device((spot + step) % n_plane)
-            start_copy(slots.at[spot], slots.at[spot], sems.at[0], sems.at[1], device)
-
-        repeat(1, n_plane, send)
-
     def plane_scatter(sources, slots, sems):
         def send(step):
             other = (spot + step) % n_plane
@@ -221,8 +207,8 @@
         if n_plane > 1:
             wait_bytes(slots.at[pl.ds(0, n_plane - 1)], sems.at[which])
 
-    def tile_of(sums):
-        rest = jnp.zeros((8 - len(sums), columns), F32)
+    def tile_of(sums, rows=8):
+        rest = jnp.zeros((rows - len(sums), columns), F32)
         return jnp.concatenate(list(sums) + [rest], axis=0)
 
     def turn(chunk):
@@ -368,7 +354,7 @@
         spread[1, face] = (weights - high.astype(F32)).astype(BF16)
     make_packs(0, right_side.astype(BF16))
 
-    pl.semaphore_wait(barrier, peers)
+    pl.semaphore_wait(barrier, n_all - 1)
     plane_scatter(pieces, solver, pieces_sem)
     send_line(0)
     send_packs(0)
@@ -406,19 +392,23 @@
     one_two = first_dot * (1.0 - one_one) / first_norm
     two_two = remainder_square / (remainder_square + EPSILON)
     image = (image - first_dot * image_one) / first_norm
-    line_sums[2, line] = tile_of(
+    all_sums[place] = tile_of(
         [
             column_sum(image * krylov_one),
             column_sum(image * krylov_two),
             column_sum(image * image),
-        ]
-    )
-    line_gather(line_sums.at[2], line_sem.at[2])
-    wait_line(line_sums.at[2], line_sem.at[2], 1)
-    plane_sums[spot] = jnp.sum(line_sums[2], axis=0)
-    plane_gather(plane_sums, plane_sem)
-    wait_plane(plane_sums, plane_sem, 1)
-    sums = jnp.sum(plane_sums[...], axis=0)
+        ],
+        4,
+    )
+
+    def send_sums(step):
+        start_copy(
+            all_sums.at[place], all_sums.at[place], all_sem.at[0], all_sem.at[1], other_device(step)
+        )
+
+    repeat(1, n_all, send_sums, 32)
+    wait_bytes(all_sums.at[pl.ds(0, n_all - 1)], all_sem.at[1])
+    sums = jnp.sum(all_sums[...], axis=0)
     cross_dot, second_dot, image_square = sums[0:1], sums[1:2], sums[2:3]
     remainder_square = (
         image_square
@@ -433,9 +423,9 @@
     out_ref[...] = weight_one * precond_one + weight_two * precond_two
     relative_ref[...] = relative
 
-    for which in range(3):
+    for which in range(2):
         wait_line(line_sums.at[which], line_sem.at[which], 0)
-    wait_plane(plane_sums, plane_sem, 0)
+    wait_bytes(all_sums.at[pl.ds(0, n_all - 1)], all_sem.at[0])
     wait_plane(solver, pieces_sem, 0)
     for which in range(2):
         wait_line(gathered.at[which], gather_sem.at[which], 0)
@@ -504,8 +494,8 @@
             pltpu.VMEM((2, n_line, width, columns), BF16),
             pltpu.VMEM((2, n_plane, width + 8, columns), F32),
             pltpu.VMEM((2, n_plane, width + 8, columns), F32),
-            pltpu.VMEM((3, n_line, 8, columns), F32),
-            pltpu.VMEM((n_plane, 8, columns), F32),
+            pltpu.VMEM((2, n_line, 8, columns), F32),
+            pltpu.VMEM((n_gx * n_gy, 4, columns), F32),
             pltpu.VMEM((4, width, margin_rows), BF16),
             pltpu.VMEM((4, width, margin_rows), BF16),
             pltpu.VMEM((owned, 8 * width), BF16),
@@ -521,7 +511,7 @@
             dma((4, 4)),
             dma((2, 2)),
             dma((2, 2)),
-            dma((3, 2)),
+            dma((2, 2)),
             dma((2,)),
         ],
         compiler_params=pltpu.CompilerParams(

time: 38.5 us -> 38 us (0.987)
  Pallas kernels: 35.7 us -> 35.1 us
    pallas_call x1, Pallas kernels: 35.7 us -> 35.1 us  [on_device(): pl.pallas_call(functools.partial(kernel, n_gx, n_gy, plane), out_shape=(j...]
where the time goes in v5:
time: 38 us; the launch traced here: 37.8 us
  Pallas kernels  35.1 us (92%)
  local copies, waits for them, and re-layouts  1.99 us (5%)
  between operations  0.65 us (2%)
    pallas_call x1, Pallas kernels, on_device(): pl.pallas_call(functools.partial(kernel, n_gx, n_gy, plane), out_shape=(j...  35.1 us
    unnamed x4, local copies, waits for them, and re-layouts  1.99 us

profile of v5, /device:TPU:0, one launch (start us, length us, event | category | flops | bytes accessed | tf_op | source)
XLA Modules:
  0.0 37.8 jit_solution(3560122978375972998)
XLA Ops:
  0.6 35.1 %shard_map.95 = (f32[128,128]{1,0:T(8,128)}, f32[1,128]{1,0:T(1,128)}) custom-call(f32[128,128]{1,0:T(8,128)} %bitcast.13, s32[4,128]{1,0:T(4,128)} %bitcast.17, f32[4,128]{1,0:T(4,128)} %bitcast.18, bf16[1,128,128]{2,1,0:T(8,128)(2,1)} %bitcast.15, bf16[128,640]{1,0:T(8,128)(2,1)} %bitcast.11, bf16[32,128]{1,0:T(8,128)(2,1)} %bitcast.16, ...), custom_call_target="tpu_custom_call" | custom-call | tf_op jit(solution)/shard_map/pallas_call | solution.py:475
  35.8 0.0 copy-start
  35.8 1.5 %copy.12 = f32[1,1,128,128]{3,2,1,0:T(8,128)} copy(f32[1,1,128,128]{3,2,1,0:T(8,128)} %bitcast.12) | data formatting | bytes 131072
  37.3 0.0 copy-done
  37.3 0.5 %copy.13 = f32[128]{0:T(128)} copy(f32[128]{0:T(128)S(1)} %bitcast.19) | data formatting | bytes 1024
Async XLA Ops:
  35.8 1.5 %copy-start = (f32[1,128]{1,0:T(1,128)S(1)}, f32[1,128]{1,0:T(1,128)}, u32[]{:S(2)}) copy-start(f32[1,128]{1,0:T(1,128)} %get-tuple-element.5) | copy-start | bytes 1540

commit v6 on v5

--- a/solution.py
+++ b/solution.py
@@ -135,15 +135,29 @@
         other = (place + step) % n_all
         return (other // n_gy, other % n_gy)
 
-    lax.fori_loop(1, n_all, lambda step, carry: (greet(other_device(step)), carry)[1], 0)
+    repeat(1, n_line, lambda step: greet(line_device((line + step) % n_line)))
+    repeat(1, n_plane, lambda step: greet(plane_device((spot + step) % n_plane)))
+    cross_down = jnp.logical_and(i % plane == 0, i > 0)
+    cross_up = jnp.logical_and(i % plane == plane - 1, i < n_gx - 1)
+    peers = n_line + n_plane - 2
+    if plane > 1:
+        peers += cross_down.astype(jnp.int32) + cross_up.astype(jnp.int32)
+
+        @pl.when(cross_down)
+        def _():
+            greet((i - 1, j))
+
+        @pl.when(cross_up)
+        def _():
+            greet((i + 1, j))
 
     operands = {}
     for index, (name, source, target) in enumerate(
         (
+            ("rhs", rhs_hbm, rhs_ref),
+            ("basis", basis_t_hbm, basis_t),
             ("coarse", coarse_hbm, coarse_ref),
             ("map", map_hbm, map_ref),
-            ("rhs", rhs_hbm, rhs_ref),
-            ("basis", basis_t_hbm, basis_t),
             ("rows", rows_hbm, rows_ref),
             ("weight", weight_hbm, weight_ref),
             ("inverse", inverse_hbm, inverse_ref),
@@ -330,16 +344,19 @@
         own -= dot(fold[...], jnp.concatenate([coarse, coarse], axis=0))
         return applied, own, total[width:]
 
+    operands["rhs"].wait()
+    operands["basis"].wait()
+    right_side = rhs_ref[...]
+    parts = halves(right_side)
+    store_line(0, parts, [column_sum(right_side * right_side)])
     operands["coarse"].wait()
     operands["map"].wait()
     repeat(0, coarse_ref.shape[1] // LANES, turn)
     repeat(0, n_plane, arrange)
-    operands["rhs"].wait()
-    operands["basis"].wait()
-    right_side = rhs_ref[...]
-    basis_ref[...] = basis_t[...].astype(F32).T.astype(BF16)
-    parts = halves(right_side)
-    store_line(0, parts, [column_sum(right_side * right_side)])
+    pl.semaphore_wait(barrier, peers)
+    send_line(0)
+    plane_scatter(pieces, solver, pieces_sem)
+    solver[spot] = pieces[spot]
     operands["rows"].wait()
     operands["weight"].wait()
     row_ids = lax.broadcasted_iota(jnp.int32, (owned, rows_ref.shape[1]), 0)
@@ -348,20 +365,18 @@
         one_hot = jnp.where(hit, 1.0, 0.0).astype(F32)
         select[face] = one_hot.T.astype(BF16)
         basis_packs[face] = dot(basis_t[...], one_hot.astype(BF16)).astype(BF16)
+    make_packs(0, right_side.astype(BF16))
+    send_packs(0)
+    send_faces(
+        [basis_packs.at[face] for face in range(4)], basis_margins, basis_send, basis_recv
+    )
+    for face in range(4):
+        hit = row_ids == rows_ref[face : face + 1, :]
         weights = jnp.where(hit, weight_ref[face : face + 1, :], 0.0)
         high = weights.astype(BF16)
         spread[0, face] = high
         spread[1, face] = (weights - high.astype(F32)).astype(BF16)
-    make_packs(0, right_side.astype(BF16))
-
-    pl.semaphore_wait(barrier, n_all - 1)
-    plane_scatter(pieces, solver, pieces_sem)
-    send_line(0)
-    send_packs(0)
-    send_faces(
-        [basis_packs.at[face] for face in range(4)], basis_margins, basis_send, basis_recv
-    )
-    solver[spot] = pieces[spot]
+    basis_ref[...] = basis_t[...].astype(F32).T.astype(BF16)
     operands["inverse"].wait()
     operands["block"].wait()
     wait_plane(solver, pieces_sem, 1)

time: 38 us -> 36.4 us (0.958)
  Pallas kernels: 35.1 us -> 33.6 us
    pallas_call x1, Pallas kernels: 35.1 us -> 33.6 us  [on_device(): pl.pallas_call(functools.partial(kernel, n_gx, n_gy, plane), out_shape=(j...]
where the time goes in v6:
time: 36.4 us; the launch traced here: 36.2 us
  Pallas kernels  33.6 us (92%)
  local copies, waits for them, and re-layouts  1.99 us (5%)
  between operations  0.65 us (2%)
    pallas_call x1, Pallas kernels, on_device(): pl.pallas_call(functools.partial(kernel, n_gx, n_gy, plane), out_shape=(j...  33.6 us
    unnamed x4, local copies, waits for them, and re-layouts  1.99 us

profile of v6, /device:TPU:0, one launch (start us, length us, event | category | flops | bytes accessed | tf_op | source)
XLA Modules:
  0.0 36.2 jit_solution(615416501406815120)
XLA Ops:
  0.6 33.6 %shard_map.95 = (f32[128,128]{1,0:T(8,128)}, f32[1,128]{1,0:T(1,128)}) custom-call(f32[128,128]{1,0:T(8,128)} %bitcast.13, s32[4,128]{1,0:T(4,128)} %bitcast.17, f32[4,128]{1,0:T(4,128)} %bitcast.18, bf16[1,128,128]{2,1,0:T(8,128)(2,1)} %bitcast.15, bf16[128,640]{1,0:T(8,128)(2,1)} %bitcast.11, bf16[32,128]{1,0:T(8,128)(2,1)} %bitcast.16, ...), custom_call_target="tpu_custom_call" | custom-call | tf_op jit(solution)/shard_map/pallas_call | solution.py:490
  34.2 0.0 copy-start
  34.3 1.5 %copy.12 = f32[1,1,128,128]{3,2,1,0:T(8,128)} copy(f32[1,1,128,128]{3,2,1,0:T(8,128)} %bitcast.12) | data formatting | bytes 131072
  35.7 0.0 copy-done
  35.7 0.5 %copy.13 = f32[128]{0:T(128)} copy(f32[128]{0:T(128)S(1)} %bitcast.19) | data formatting | bytes 1024
Async XLA Ops:
  34.2 1.5 %copy-start = (f32[1,128]{1,0:T(1,128)S(1)}, f32[1,128]{1,0:T(1,128)}, u32[]{:S(2)}) copy-start(f32[1,128]{1,0:T(1,128)} %get-tuple-element.5) | copy-start | bytes 1540

commit v7 on v6

--- a/solution.py
+++ b/solution.py
@@ -305,11 +305,15 @@
             solver[...].reshape(n_plane * width, n_line * width),
             gathered[which].reshape(n_line * width, columns),
         ).reshape(n_plane, width, columns)
-        partial[which, :, :width, :] = products
+        partial[which, :, :width, :] = products.astype(BF16)
         wait_line(line_sums.at[which], line_sem.at[which], 1)
-        line_total = jnp.sum(line_sums[which], axis=0)
+        line_total = jnp.sum(line_sums[which], axis=0)[:4]
+        high = line_total.astype(BF16).astype(F32)
+        middle = (line_total - high).astype(BF16).astype(F32)
+        low = line_total - high - middle
+        packed = jnp.concatenate([high, middle, low, jnp.zeros_like(low)], axis=0).astype(BF16)
         for member in range(n_plane):
-            partial[which, member, width:, :] = line_total
+            partial[which, member, width:, :] = packed
         plane_scatter(partial.at[which], received.at[which], partial_sem.at[which])
         received[which, spot] = partial[which, spot]
         wait_margins(2 * which)
@@ -319,7 +323,8 @@
         if which == 0:
             fold_basis()
         wait_plane(received.at[which], partial_sem.at[which], 1)
-        total = jnp.sum(received[which], axis=0)
+        total = jnp.sum(received[which].astype(F32), axis=0)
+        packed = total[width:]
         solved[which] = total[:width].astype(BF16)
         send_faces(
             [solved.at[which]] * 4,
@@ -342,7 +347,7 @@
         wait_faces(solved_margins.at[which], solved_recv.at[which])
         coarse = solved_margins[which].reshape(4 * width, columns)
         own -= dot(fold[...], jnp.concatenate([coarse, coarse], axis=0))
-        return applied, own, total[width:]
+        return applied, own, packed[0:4] + packed[4:8] + packed[8:12]
 
     operands["rhs"].wait()
     operands["basis"].wait()
@@ -507,8 +512,8 @@
             pltpu.VMEM((4, 4, margin_rows, columns), BF16),
             pltpu.VMEM((4, 4, margin_rows, columns), BF16),
             pltpu.VMEM((2, n_line, width, columns), BF16),
-            pltpu.VMEM((2, n_plane, width + 8, columns), F32),
-            pltpu.VMEM((2, n_plane, width + 8, columns), F32),
+            pltpu.VMEM((2, n_plane, width + 16, columns), BF16),
+            pltpu.VMEM((2, n_plane, width + 16, columns), BF16),
             pltpu.VMEM((2, n_line, 8, columns), F32),
             pltpu.VMEM((n_gx * n_gy, 4, columns), F32),
             pltpu.VMEM((4, width, margin_rows), BF16),

time: 36.4 us -> 35.4 us (0.973)
  Pallas kernels: 33.6 us -> 32.6 us
    pallas_call x1, Pallas kernels: 33.6 us -> 32.6 us  [on_device(): pl.pallas_call(functools.partial(kernel, n_gx, n_gy, plane), out_shape=(j...]
where the time goes in v7:
time: 35.4 us; the launch traced here: 35.2 us
  Pallas kernels  32.6 us (92%)
  local copies, waits for them, and re-layouts  1.99 us (6%)
  between operations  0.65 us (2%)
    pallas_call x1, Pallas kernels, on_device(): pl.pallas_call(functools.partial(kernel, n_gx, n_gy, plane), out_shape=(j...  32.6 us
    unnamed x4, local copies, waits for them, and re-layouts  1.99 us

profile of v7, /device:TPU:0, one launch (start us, length us, event | category | flops | bytes accessed | tf_op | source)
XLA Modules:
  0.0 35.2 jit_solution(11262527329811127332)
XLA Ops:
  0.6 32.6 %shard_map.95 = (f32[128,128]{1,0:T(8,128)}, f32[1,128]{1,0:T(1,128)}) custom-call(f32[128,128]{1,0:T(8,128)} %bitcast.13, s32[4,128]{1,0:T(4,128)} %bitcast.17, f32[4,128]{1,0:T(4,128)} %bitcast.18, bf16[1,128,128]{2,1,0:T(8,128)(2,1)} %bitcast.15, bf16[128,640]{1,0:T(8,128)(2,1)} %bitcast.11, bf16[32,128]{1,0:T(8,128)(2,1)} %bitcast.16, ...), custom_call_target="tpu_custom_call" | custom-call | tf_op jit(solution)/shard_map/pallas_call | solution.py:495
  33.2 0.0 copy-start
  33.2 1.5 %copy.12 = f32[1,1,128,128]{3,2,1,0:T(8,128)} copy(f32[1,1,128,128]{3,2,1,0:T(8,128)} %bitcast.12) | data formatting | bytes 131072
  34.7 0.0 copy-done
  34.7 0.5 %copy.13 = f32[128]{0:T(128)} copy(f32[128]{0:T(128)S(1)} %bitcast.19) | data formatting | bytes 1024
Async XLA Ops:
  33.2 1.5 %copy-start = (f32[1,128]{1,0:T(1,128)S(1)}, f32[1,128]{1,0:T(1,128)}, u32[]{:S(2)}) copy-start(f32[1,128]{1,0:T(1,128)} %get-tuple-element.5) | copy-start | bytes 1540

commit v8 on v7

--- a/solution.py
+++ b/solution.py
@@ -88,7 +88,6 @@
     gathered,
     partial,
     received,
-    line_sums,
     all_sums,
     basis_packs,
     basis_margins,
@@ -105,7 +104,6 @@
     margin_recv,
     gather_sem,
     partial_sem,
-    line_sem,
     all_sem,
 ):
     i = lax.axis_index("gx")
@@ -221,7 +219,7 @@
         if n_plane > 1:
             wait_bytes(slots.at[pl.ds(0, n_plane - 1)], sems.at[which])
 
-    def tile_of(sums, rows=8):
+    def tile_of(sums, rows):
         rest = jnp.zeros((rows - len(sums), columns), F32)
         return jnp.concatenate(list(sums) + [rest], axis=0)
 
@@ -273,13 +271,21 @@
     def wait_margins(exchange):
         wait_faces(margins.at[exchange], margin_recv.at[exchange])
 
+    def packed(sums):
+        high = sums.astype(BF16).astype(F32)
+        middle = (sums - high).astype(BF16).astype(F32)
+        low = sums - high - middle
+        return jnp.concatenate([high, middle, low, jnp.zeros_like(low)], axis=0).astype(BF16)
+
+    def unpacked(rows):
+        return rows[0:4] + rows[4:8] + rows[8:12]
+
     def store_line(which, parts, sums):
-        gathered[which, line] = joined(dot(basis_t[...], parts)).astype(BF16)
-        line_sums[which, line] = tile_of(sums)
+        gathered[which, line, :width, :] = joined(dot(basis_t[...], parts)).astype(BF16)
+        gathered[which, line, width:, :] = packed(tile_of(sums, 4))
 
     def send_line(which):
         line_gather(gathered.at[which], gather_sem.at[which])
-        line_gather(line_sums.at[which], line_sem.at[which])
 
     def fold_basis():
         wait_faces(basis_margins, basis_recv)
@@ -303,17 +309,14 @@
         wait_line(gathered.at[which], gather_sem.at[which], 1)
         products = dot(
             solver[...].reshape(n_plane * width, n_line * width),
-            gathered[which].reshape(n_line * width, columns),
+            gathered[which, :, :width, :].reshape(n_line * width, columns),
         ).reshape(n_plane, width, columns)
         partial[which, :, :width, :] = products.astype(BF16)
-        wait_line(line_sums.at[which], line_sem.at[which], 1)
-        line_total = jnp.sum(line_sums[which], axis=0)[:4]
-        high = line_total.astype(BF16).astype(F32)
-        middle = (line_total - high).astype(BF16).astype(F32)
-        low = line_total - high - middle
-        packed = jnp.concatenate([high, middle, low, jnp.zeros_like(low)], axis=0).astype(BF16)
+        line_total = packed(
+            unpacked(jnp.sum(gathered[which, :, width:, :].astype(F32), axis=0))
+        )
         for member in range(n_plane):
-            partial[which, member, width:, :] = packed
+            partial[which, member, width:, :] = line_total
         plane_scatter(partial.at[which], received.at[which], partial_sem.at[which])
         received[which, spot] = partial[which, spot]
         wait_margins(2 * which)
@@ -324,7 +327,6 @@
             fold_basis()
         wait_plane(received.at[which], partial_sem.at[which], 1)
         total = jnp.sum(received[which].astype(F32), axis=0)
-        packed = total[width:]
         solved[which] = total[:width].astype(BF16)
         send_faces(
             [solved.at[which]] * 4,
@@ -347,7 +349,7 @@
         wait_faces(solved_margins.at[which], solved_recv.at[which])
         coarse = solved_margins[which].reshape(4 * width, columns)
         own -= dot(fold[...], jnp.concatenate([coarse, coarse], axis=0))
-        return applied, own, packed[0:4] + packed[4:8] + packed[8:12]
+        return applied, own, unpacked(total[width:])
 
     operands["rhs"].wait()
     operands["basis"].wait()
@@ -443,8 +445,6 @@
     out_ref[...] = weight_one * precond_one + weight_two * precond_two
     relative_ref[...] = relative
 
-    for which in range(2):
-        wait_line(line_sums.at[which], line_sem.at[which], 0)
     wait_bytes(all_sums.at[pl.ds(0, n_all - 1)], all_sem.at[0])
     wait_plane(solver, pieces_sem, 0)
     for which in range(2):
@@ -511,10 +511,9 @@
             pltpu.VMEM((owned, width), BF16),
             pltpu.VMEM((4, 4, margin_rows, columns), BF16),
             pltpu.VMEM((4, 4, margin_rows, columns), BF16),
-            pltpu.VMEM((2, n_line, width, columns), BF16),
+            pltpu.VMEM((2, n_line, width + 16, columns), BF16),
             pltpu.VMEM((2, n_plane, width + 16, columns), BF16),
             pltpu.VMEM((2, n_plane, width + 16, columns), BF16),
-            pltpu.VMEM((2, n_line, 8, columns), F32),
             pltpu.VMEM((n_gx * n_gy, 4, columns), F32),
             pltpu.VMEM((4, width, margin_rows), BF16),
             pltpu.VMEM((4, width, margin_rows), BF16),
@@ -531,7 +530,6 @@
             dma((4, 4)),
             dma((2, 2)),
             dma((2, 2)),
-            dma((2, 2)),
             dma((2,)),
         ],
         compiler_params=pltpu.CompilerParams(

time: 35.4 us -> 35.3 us (level)
  no operation moved by 1% of the time
where the time goes in v8:
time: 35.3 us; the launch traced here: 35.2 us
  Pallas kernels  32.5 us (92%)
  local copies, waits for them, and re-layouts  1.99 us (6%)
  between operations  0.65 us (2%)
    pallas_call x1, Pallas kernels, on_device(): pl.pallas_call(functools.partial(kernel, n_gx, n_gy, plane), out_shape=(j...  32.5 us
    unnamed x4, local copies, waits for them, and re-layouts  1.99 us

profile of v8, /device:TPU:0, one launch (start us, length us, event | category | flops | bytes accessed | tf_op | source)
XLA Modules:
  0.0 35.2 jit_solution(3021419570410454572)
XLA Ops:
  0.6 32.5 %shard_map.95 = (f32[128,128]{1,0:T(8,128)}, f32[1,128]{1,0:T(1,128)}) custom-call(f32[128,128]{1,0:T(8,128)} %bitcast.13, s32[4,128]{1,0:T(4,128)} %bitcast.17, f32[4,128]{1,0:T(4,128)} %bitcast.18, bf16[1,128,128]{2,1,0:T(8,128)(2,1)} %bitcast.15, bf16[128,640]{1,0:T(8,128)(2,1)} %bitcast.11, bf16[32,128]{1,0:T(8,128)(2,1)} %bitcast.16, ...), custom_call_target="tpu_custom_call" | custom-call | tf_op jit(solution)/shard_map/pallas_call | solution.py:495
  33.2 0.0 copy-start
  33.2 1.5 %copy.12 = f32[1,1,128,128]{3,2,1,0:T(8,128)} copy(f32[1,1,128,128]{3,2,1,0:T(8,128)} %bitcast.12) | data formatting | bytes 131072
  34.6 0.0 copy-done
  34.6 0.5 %copy.13 = f32[128]{0:T(128)} copy(f32[128]{0:T(128)S(1)} %bitcast.19) | data formatting | bytes 1024
Async XLA Ops:
  33.2 1.5 %copy-start = (f32[1,128]{1,0:T(1,128)S(1)}, f32[1,128]{1,0:T(1,128)}, u32[]{:S(2)}) copy-start(f32[1,128]{1,0:T(1,128)} %get-tuple-element.5) | copy-start | bytes 1540
